TPU v7x, 32 devices: a whole 2x2x4 slice. The times are simulated.
32 devices in a mesh: ctx: 4 (over y, x), tp: 8 (over z, core).
Axes of the slice: x: 2, y: 2, z: 4, core: 2. Of those that a mesh axis runs over, the one named last changes fastest.
Arguments:
- normed_rows: bfloat16 [3072, 4096], P(('ctx', 'tp')), may hold values from -6 to 6
- out_grad: bfloat16 [3072, 4096], P(('ctx', 'tp')), may hold values from -6 to 6
- inner_weight: bfloat16 [2, 4096, 2048], P(None, None, 'tp'), may hold values from -0.09375 to 0.09375
- state_weight: bfloat16 [4096, 256], replicated, may hold values from -0.09375 to 0.09375
- step_weight: bfloat16 [4096, 16], P(None, 'tp'), may hold values from -0.09375 to 0.09375
- conv_inner: float32 [4, 2048], P(None, 'tp'), may hold values from -3 to 3
- conv_state: float32 [4, 256], replicated, may hold values from -3 to 3
- step_bias: float32 [16], P('tp'), may hold values from -4 to -1
- decay_log: float32 [16], P('tp')
- norm_gain: float32 [2048], P('tp'), may hold values from 0.1 to 1.9
- out_weight: bfloat16 [2048, 4096], P('tp'), may hold values from -0.125 to 0.125
Outputs:
- input_grad: bfloat16 [3072, 4096], P(('ctx', 'tp'))
All inputs are finite; a program needn't handle non-finite values.
Results may differ from a plain program's by a relative error of at most 0.0095.
Values may be sent and summed in bfloat16 or wider, within the bound.
No kernel may reach another device: no remote copies, remote signals or barrier semaphores. Data moves between devices by JAX's collectives and lax.ppermute only.
A program may use at most 128 MiB of HBM per device.

v0:
```python
import math
from functools import partial

import jax
import jax.numpy as jnp
from jax import lax
from jax.experimental import pallas as pl
from jax.experimental.pallas import tpu as pltpu
from jax.sharding import PartitionSpec as P

HEAD_DIM = 128
STATE = 128
CONV = 4
LANES = 128
PAD = 8
EPSILON = 1e-05
EXACT = lax.Precision.HIGHEST
F32 = jnp.float32
BF16 = jnp.bfloat16
COST = pl.CostEstimate(flops=1000, bytes_accessed=1000, transcendentals=0)
VMEM_LIMIT = 16 * 1024 * 1024
PARAMS = dict(
    compiler_params=pltpu.CompilerParams(vmem_limit_bytes=16 * 1024 * 1024), cost_estimate=COST
)


def dot(a, b, over=(1, 0), precision=None):
    return lax.dot_general(
        a, b, (((over[0],), (over[1],)), ((), ())), precision=precision, preferred_element_type=F32
    )


def triangle(size, keep):
    rows = lax.broadcasted_iota(jnp.int32, (size, size), 0)
    columns = lax.broadcasted_iota(jnp.int32, (size, size), 1)
    return keep(rows, columns)


def head(h):
    return slice(h * HEAD_DIM, (h + 1) * HEAD_DIM)


def forward_local(
    heads, block, proj, tail, kern, bias, rate,
    act_out, scaled_out, slope_out, step_out, run_out, sig_out, decay_out, table_out, diag_out, states_out,
    own_out, ext,
):
    length = proj.shape[0]
    width = heads * HEAD_DIM
    conv_width = width + 2 * STATE
    ext[0:PAD, :] = tail[...].astype(F32)
    ext[PAD:, :] = proj[:, width : width + conv_width].astype(F32)
    causal = triangle(block, lambda i, j: i >= j)
    lower = causal.astype(F32)
    state = [jnp.zeros((HEAD_DIM, STATE), F32) for _ in range(heads)]
    for k in range(length // block):
        rows = slice(k * block, (k + 1) * block)
        first = k * block + PAD - (CONV - 1)
        value = kern[0:1, :] * ext[first : first + block, :]
        for j in range(1, CONV):
            value = value + kern[j : j + 1, :] * ext[first + j : first + j + block, :]
        sigmoid = 1.0 / (1.0 + jnp.exp(-value))
        act = value * sigmoid
        act_out[rows, :] = act.astype(BF16)
        slope_out[rows, :] = sigmoid * (1.0 + value * (1.0 - sigmoid))
        raw = proj[rows, width + conv_width :].astype(F32) + bias[...]
        grown = jnp.exp(-jnp.abs(raw))
        step = jnp.maximum(raw, 0.0) + jnp.log1p(grown)
        step_out[rows, :] = step
        sig_out[rows, :] = jnp.where(raw >= 0.0, 1.0, grown) / (1.0 + grown)
        run = dot(lower, -step * rate[...], precision=EXACT)
        run_out[rows, :] = run
        run_t = run.T
        b_rows = act[:, width : width + STATE]
        c_rows = act[:, width + STATE :]
        scores = dot(c_rows, b_rows, (1, 1), EXACT)
        for h in range(heads):
            at = k * heads + h
            col = run[:, h : h + 1]
            decay = jnp.where(causal, jnp.exp(jnp.minimum(col - run_t[h : h + 1, :], 0.0)), 0.0)
            table = decay * scores
            scaled = act[:, head(h)] * step[:, h : h + 1]
            scaled_out[rows, head(h)] = scaled.astype(BF16)
            decay_out[rows, head(h)] = decay.astype(BF16)
            table_out[rows, head(h)] = table.astype(BF16)
            diag_out[rows, head(h)] = dot(table, scaled, precision=EXACT)
            states_out[at * HEAD_DIM : (at + 1) * HEAD_DIM, :] = state[h]
            last = run[block - 1 : block, h : h + 1]
            state[h] = jnp.exp(last) * state[h] + dot(
                jnp.exp(last - col) * scaled, b_rows, (0, 0), EXACT
            )
    for h in range(heads):
        own_out[head(h), :] = state[h]


def forward_carried(
    heads, block, proj, act, run, diag, states, weights, *refs,
):
    received = refs[:-6]
    gated_out, silu_out, slope_out, carried_out, states_out, sums_out = refs[-6:]
    length = proj.shape[0]
    width = heads * HEAD_DIM
    entering = []
    for h in range(heads):
        total = jnp.zeros((HEAD_DIM, STATE), F32)
        for i, part in enumerate(received):
            total = total + weights[i * heads + h : i * heads + h + 1, :] * part[head(h), :]
        entering.append(total)
    base = jnp.zeros((1, LANES), F32)
    ones = jnp.ones((8, width), F32)
    for k in range(length // block):
        rows = slice(k * block, (k + 1) * block)
        r = run[rows, :]
        grow = jnp.exp(r)
        reach = jnp.exp(base)
        c_rows = act[rows, width + STATE :].astype(F32)
        for h in range(heads):
            at = k * heads + h
            here = slice(at * HEAD_DIM, (at + 1) * HEAD_DIM)
            state = states[here, :] + reach[:, h : h + 1] * entering[h]
            states_out[here, :] = state.astype(BF16)
            carried = grow[:, h : h + 1] * dot(c_rows, state, (1, 1), EXACT)
            carried_out[rows, head(h)] = carried.astype(BF16)
            out = diag[rows, head(h)] + carried
            gate = proj[rows, head(h)].astype(F32)
            sigmoid = 1.0 / (1.0 + jnp.exp(-gate))
            silu = gate * sigmoid
            silu_out[rows, head(h)] = silu
            gated_out[rows, head(h)] = out * silu
            slope_out[rows, head(h)] = out * sigmoid * (1.0 + gate * (1.0 - sigmoid))
        base = base + r[block - 1 : block, :]
        gated = gated_out[rows, :]
        sums_out[:, rows] = dot(ones, gated * gated, (1, 1), EXACT)


def token_sums(local, gain, gated, squares, sums_out):
    ones = jnp.ones((8, local.shape[1]), F32)
    cross = dot(ones, gain[...] * local[...] * gated[...], (1, 1), EXACT)
    upper = lax.broadcasted_iota(jnp.int32, cross.shape, 0) < 4
    sums_out[...] = jnp.where(upper, squares[...], cross)


def backward_gate(heads, block, total_width, local, gain, gated, silu, slope, act, run, *refs):
    parts = refs[:-5]
    dgate_out, cot_out, grown_out, blocks_out, own_out = refs[-5:]
    length = local.shape[0]
    width = heads * HEAD_DIM
    pick = lax.broadcasted_iota(jnp.int32, (8, LANES), 0)
    own = [jnp.zeros((HEAD_DIM, STATE), F32) for _ in range(heads)]
    base = jnp.zeros((1, LANES), F32)
    for k in range(length // block):
        rows = slice(k * block, (k + 1) * block)
        sums = parts[0][:, rows]
        for part in parts[1:]:
            sums = sums + part[:, rows]
        square = dot(sums, (pick == 0).astype(F32), (0, 0), EXACT) / total_width
        cross = dot(sums, (pick == 4).astype(F32), (0, 0), EXACT) / total_width
        inverse = lax.rsqrt(square + EPSILON)
        cross = cross * (inverse * inverse * inverse)
        r = run[rows, :]
        grow = jnp.exp(r)
        reach = jnp.exp(base)
        c_rows = act[rows, width + STATE :]
        for h in range(heads):
            at = k * heads + h
            d_gated = inverse * (gain[:, head(h)] * local[rows, head(h)]) - gated[rows, head(h)] * cross
            dgate_out[rows, head(h)] = (d_gated * slope[rows, head(h)]).astype(BF16)
            cot = d_gated * silu[rows, head(h)]
            cot_out[rows, head(h)] = cot.astype(BF16)
            grown = (grow[:, h : h + 1] * cot).astype(BF16)
            grown_out[rows, head(h)] = grown
            entering = dot(grown, c_rows, (0, 0))
            blocks_out[at * HEAD_DIM : (at + 1) * HEAD_DIM, :] = entering
            own[h] = own[h] + reach[:, h : h + 1] * entering
        base = base + r[block - 1 : block, :]
    for h in range(heads):
        own_out[head(h), :] = own[h]


def backward_local(
    heads, block, cot, grown, act, scaled, decays, table, states, carried, u_out, dbc_out, decay_out
):
    length = cot.shape[0]
    width = heads * HEAD_DIM
    before = triangle(block, lambda i, j: i > j)
    upper = triangle(block, lambda i, j: i <= j).astype(BF16)
    lane = lax.broadcasted_iota(jnp.int32, (block, LANES), 1)
    for k in range(length // block):
        rows = slice(k * block, (k + 1) * block)
        b_rows = act[rows, width : width + STATE]
        c_rows = act[rows, width + STATE :]
        d_brows = jnp.zeros((block, STATE), F32)
        d_crows = jnp.zeros((block, STATE), F32)
        decay = jnp.zeros((block, LANES), F32)
        for h in range(heads):
            at = k * heads + h
            g = cot[rows, head(h)]
            weights = table[rows, head(h)]
            inner = dot(g, scaled[rows, head(h)], (1, 1))
            pairs = (decays[rows, head(h)].astype(F32) * inner).astype(BF16)
            mixed = (weights.astype(F32) * inner).astype(BF16)
            d_crows = d_crows + dot(pairs, b_rows)
            d_crows = d_crows + dot(grown[rows, head(h)], states[at * HEAD_DIM : (at + 1) * HEAD_DIM, :])
            d_brows = d_brows + dot(pairs, c_rows, (0, 0))
            u_out[rows, head(h)] = dot(weights, g, (0, 0))
            through = (g.astype(F32) * carried[rows, head(h)].astype(F32)).astype(BF16)
            spread = jnp.where(before, dot(upper, mixed), 0.0) + dot(upper, through)
            decay = jnp.where(lane == h, jnp.sum(spread, axis=1, keepdims=True), decay)
        dbc_out[rows, :STATE] = d_brows
        dbc_out[rows, STATE:] = d_crows
        decay_out[rows, :] = decay


def backward_carried(
    heads, block, dgate, act, scaled, slope, step, run, sig, rate, kern, states, blocks, u, dbc, decay, weights,
    *refs,
):
    received = refs[:-4]
    cat_out, end_out, tail_out, scr = refs[-4:]
    length = dgate.shape[0]
    width = heads * HEAD_DIM
    conv_width = width + 2 * STATE
    strict = triangle(block, lambda i, j: i > j).astype(BF16)
    lane = lax.broadcasted_iota(jnp.int32, (block, LANES), 1)
    scr[0:PAD, :] = jnp.zeros((PAD, conv_width), F32)
    scr[PAD + length :, :] = jnp.zeros((PAD, conv_width), F32)
    cat_out[:, :width] = dgate[...]
    leaving = []
    for h in range(heads):
        total = jnp.zeros((HEAD_DIM, STATE), F32)
        for i, part in enumerate(received):
            total = total + weights[i * heads + h : i * heads + h + 1, :] * part[head(h), :]
        leaving.append(total)
    for k in reversed(range(length // block)):
        rows = slice(k * block, (k + 1) * block)
        into = slice(PAD + k * block, PAD + (k + 1) * block)
        r = run[rows, :]
        last = r[block - 1 : block, :]
        shrink = jnp.exp(last - r)
        whole = jnp.exp(last)
        b_rows = act[rows, width : width + STATE]
        d_brows = dbc[rows, :STATE]
        d_step = jnp.zeros((block, LANES), F32)
        for h in range(heads):
            at = k * heads + h
            here = slice(at * HEAD_DIM, (at + 1) * HEAD_DIM)
            cot_state = leaving[h].astype(BF16)
            past = shrink[:, h : h + 1] * dot(b_rows, cot_state, (1, 1))
            total = u[rows, head(h)] + past
            moved = scaled[rows, head(h)].astype(F32)
            d_brows = d_brows + dot((shrink[:, h : h + 1] * moved).astype(BF16), cot_state)
            kept = whole[:, h : h + 1] * leaving[h]
            constant = jnp.sum(
                jnp.sum(kept * states[here, :].astype(F32), axis=1, keepdims=True), axis=0, keepdims=True
            )
            spread = dot(strict, (moved * past).astype(BF16))
            d_decay = jnp.sum(spread, axis=1, keepdims=True) + constant + decay[rows, h : h + 1]
            direct = jnp.sum(act[rows, head(h)].astype(F32) * total, axis=1, keepdims=True)
            d_step = jnp.where(lane == h, direct - rate[:, h : h + 1] * d_decay, d_step)
            scr[into, head(h)] = step[rows, h : h + 1] * total * slope[rows, head(h)]
            leaving[h] = kept + blocks[here, :]
        scr[into, width : width + STATE] = d_brows * slope[rows, width : width + STATE]
        scr[into, width + STATE :] = dbc[rows, STATE:] * slope[rows, width + STATE :]
        cat_out[rows, width + conv_width :] = (d_step * sig[rows, :]).astype(BF16)
        value = kern[CONV - 1 : CONV, :] * scr[into, :]
        for j in range(1, CONV):
            value = value + kern[CONV - 1 - j : CONV - j, :] * scr[into.start + j : into.stop + j, :]
        cat_out[rows, width : width + conv_width] = value.astype(BF16)
        if k == length // block - 1:
            end_out[...] = value[block - PAD :, :]
    value = kern[CONV - 1 : CONV, :] * scr[0:PAD, :]
    for j in range(1, CONV):
        value = value + kern[CONV - 1 - j : CONV - j, :] * scr[j : PAD + j, :]
    tail_out[...] = value


def turned(value, axis, by):
    length = lax.axis_size(axis)
    return lax.ppermute(value, axis, [(i, (i + by) % length) for i in range(length)])


def paired(value, by):
    length = lax.axis_size("tp")
    return lax.ppermute(value, "tp", [(i, i ^ by) for i in range(length)])


def shifted(value, axis, by):
    length = lax.axis_size(axis)
    pairs = [(i, i + by) for i in range(length) if 0 <= i + by < length]
    return lax.ppermute(value, axis, pairs)


def after(value, token):
    columns = value.shape[1] if value.shape[1] <= token.shape[1] else 1
    return value + (token[:1, :columns] * 0).astype(value.dtype)


def halves(held):
    return ((0, held // 2), (held // 2, held - held // 2))


def ring_gather(parts, consume, result):
    chips = lax.axis_size("tp") // 2
    index = lax.axis_index("tp")
    chip, core = index // 2, index % 2
    arrived = []
    for step in range(chips):
        beside = [paired(part, 1) for part in parts]
        source = (chip - step) % chips
        owners = (source * 2 + core, source * 2 + 1 - core)
        if step < chips - 1:
            following = [turned(part, "tp", 2) for part in parts]
            result = consume(result, parts + beside, owners, None)
            parts = following
            arrived.append(parts)
        else:
            for i in range(len(parts)):
                result = consume(result, [parts[i], beside[i]], owners, i)
    return result, arrived


def multiply_into(weight, over, held, dtype):
    cuts = halves(held)

    def consume(result, rows, owners, only):
        product = dot(jnp.concatenate(rows, axis=0), weight, over).astype(dtype)
        at, size = (0, held) if only is None else cuts[only]
        for i, owner in enumerate(owners):
            piece = product[i * size : (i + 1) * size]
            result = lax.dynamic_update_slice(result, piece, (owner * held + at, 0))
        return result

    return consume


def product_rows(rows, weight, beside_out, mine_out):
    product = dot(rows[...], weight[...], (1, 1)).astype(BF16)
    count = beside_out.shape[0]
    beside_out[...] = product[:count]
    mine_out[...] = product[count:]


def multiply_rows(rows, weight):
    depth, inner = weight.shape
    block = math.gcd(depth, 512)
    count = rows.shape[0] // 2
    out = pl.BlockSpec((count, block), lambda i: (0, i))
    return pl.pallas_call(
        product_rows,
        grid=(depth // block,),
        in_specs=[pl.BlockSpec(rows.shape, lambda i: (0, 0)), pl.BlockSpec((block, inner), lambda i: (i, 0))],
        out_specs=[out, out],
        out_shape=[shape(count, depth, dtype=BF16)] * 2,
        name="product_rows",
        compiler_params=pltpu.CompilerParams(vmem_limit_bytes=VMEM_LIMIT),
        cost_estimate=COST,
    )(rows, weight)


def ring_scatter(cat_parts, weight, held):
    chips = lax.axis_size("tp") // 2
    index = lax.axis_index("tp")
    chip, core = index // 2, index % 2
    inner = weight.shape[1]
    shares = []
    totals = []
    for cat, (at, size) in zip(cat_parts, halves(held)):
        rows = [
            lax.dynamic_slice(cat, ((((chip - 1 - step) % chips) * 2 + side) * held + at, 0), (size, inner))
            for side in (1 - core, core)
            for step in range(chips)
        ]
        other, own = multiply_rows(jnp.concatenate(rows, axis=0), weight)
        beside = paired(other, 1)
        shares.append((own, beside))
        totals.append((own[:size].astype(F32) + beside[:size].astype(F32)).astype(BF16))
    started = list(totals)
    for step in range(1, chips):
        for i, (at, size) in enumerate(halves(held)):
            own, beside = [share[step * size : (step + 1) * size].astype(F32) for share in shares[i]]
            if step == 1 and i == 0:
                own = after(own, started[1])
            totals[i] = (own + beside + turned(totals[i], "tp", 2).astype(F32)).astype(BF16)
    return jnp.concatenate(totals, axis=0)


def shape(*dims, dtype=F32):
    return jax.ShapeDtypeStruct(dims, dtype)


def body(
    normed_rows, out_grad, inner_weight, state_weight, step_weight, conv_inner, conv_state,
    step_bias, decay_log, norm_gain, out_weight,
):
    width = inner_weight.shape[2]
    heads = step_bias.shape[0]
    members = lax.axis_size("tp")
    shards = lax.axis_size("ctx")
    mine = lax.axis_index("ctx")
    length = normed_rows.shape[0] * members
    block = math.gcd(length, 128)
    count = length // block
    conv_width = width + 2 * STATE

    weight_cat = jnp.concatenate(
        [inner_weight[0], inner_weight[1], state_weight, jnp.pad(step_weight, ((0, 0), (0, LANES - heads)))],
        axis=1,
    )
    kern = jnp.concatenate([conv_inner, conv_state], axis=1)
    bias = jnp.pad(step_bias, (0, LANES - heads))[None]
    rate = jnp.pad(jnp.exp(decay_log), (0, LANES - heads))[None]
    gain = norm_gain[None]

    held, depth = normed_rows.shape
    cuts = halves(held)
    proj, rows_in = ring_gather(
        [normed_rows[at : at + size] for at, size in cuts],
        multiply_into(weight_cat, (1, 0), held, BF16),
        jnp.zeros((length, weight_cat.shape[1]), BF16),
    )
    local, grads_in = ring_gather(
        [after(out_grad[at : at + size], rows_in[-1][i]) for i, (at, size) in enumerate(cuts)],
        multiply_into(out_weight, (1, 1), held, F32),
        jnp.zeros((length, width), F32),
    )

    tail = shifted(proj[length - PAD :, width : width + conv_width], "ctx", 1)
    act, scaled, slope, step, run, sig, decays, table, diag, states, own = pl.pallas_call(
        partial(forward_local, heads, block),
        out_shape=[
            shape(length, conv_width, dtype=BF16),
            shape(length, width, dtype=BF16),
            shape(length, conv_width),
            shape(length, LANES),
            shape(length, LANES),
            shape(length, LANES),
            shape(length, heads * block, dtype=BF16),
            shape(length, heads * block, dtype=BF16),
            shape(length, width),
            shape(count * heads * HEAD_DIM, STATE),
            shape(heads * HEAD_DIM, STATE),
        ],
        scratch_shapes=[pltpu.VMEM((PAD + length, conv_width), F32)],
        name="forward_local",
        **PARAMS,
    )(proj, tail, kern, bias, rate)

    ends = run.reshape(count, block, LANES)[:, block - 1, :heads]
    total_log = jnp.sum(ends, axis=0)
    message = jnp.concatenate([own, jnp.broadcast_to(jnp.pad(total_log, (0, LANES - heads)), (8, LANES))], axis=0)
    second = grads_in[min(1, len(grads_in) - 1)]
    message = after(message, second[0])
    received = [turned(message, "ctx", by) for by in range(1, shards)]
    logs = [part[heads * HEAD_DIM, :heads] for part in received]
    entering_weights = []
    between = jnp.zeros((heads,), F32)
    for by in range(1, shards):
        entering_weights.append(jnp.where(mine >= by, jnp.exp(between), 0.0))
        between = between + jnp.where(mine >= by, logs[by - 1], 0.0)
    leaving_weights = []
    between = jnp.zeros((heads,), F32)
    for by in range(1, shards):
        leaving_weights.append(jnp.where(mine + by < shards, jnp.exp(between), 0.0))
        between = between + jnp.where(mine + by < shards, logs[shards - by - 1], 0.0)

    def spread(parts):
        flat = jnp.concatenate(parts)
        return jnp.broadcast_to(flat[:, None], (flat.shape[0], LANES))

    gated, silu, gate_slope, carried, full_states, squares = pl.pallas_call(
        partial(forward_carried, heads, block),
        out_shape=[
            shape(length, width),
            shape(length, width),
            shape(length, width),
            shape(length, width, dtype=BF16),
            shape(count * heads * HEAD_DIM, STATE, dtype=BF16),
            shape(8, length),
        ],
        name="forward_carried",
        **PARAMS,
    )(proj, act, run, diag, states, after(spread(entering_weights), second[1]), *received)

    sums = pl.pallas_call(token_sums, out_shape=shape(8, length), name="token_sums", **PARAMS)(
        local, gain, gated, squares
    )

    sums = sums + paired(sums, 1)
    parts = [sums] + [turned(sums, "tp", by) for by in range(2, members, 2)]

    dgate, cot, grown, blocks, own_cot = pl.pallas_call(
        partial(backward_gate, heads, block, width * members),
        out_shape=[
            shape(length, width, dtype=BF16),
            shape(length, width, dtype=BF16),
            shape(length, width, dtype=BF16),
            shape(count * heads * HEAD_DIM, STATE),
            shape(heads * HEAD_DIM, STATE),
        ],
        name="backward_gate",
        **PARAMS,
    )(local, gain, gated, silu, gate_slope, act, run, *parts)

    returned = [turned(own_cot, "ctx", -by) for by in range(1, shards)]

    u, dbc, decay = pl.pallas_call(
        partial(backward_local, heads, block),
        out_shape=[shape(length, width), shape(length, 2 * STATE), shape(length, LANES)],
        name="backward_local",
        **PARAMS,
    )(cot, grown, act, scaled, decays, table, full_states, carried)

    cat, end, tail_cot = pl.pallas_call(
        partial(backward_carried, heads, block),
        out_shape=[
            shape(length, width + conv_width + LANES, dtype=BF16),
            shape(PAD, conv_width),
            shape(PAD, conv_width),
        ],
        scratch_shapes=[pltpu.VMEM((length + 2 * PAD, conv_width), F32)],
        name="backward_carried",
        **PARAMS,
    )(
        dgate, act, scaled, slope, step, run, sig, rate, kern, full_states, blocks, u, dbc, decay,
        spread(leaving_weights), *returned,
    )

    incoming = shifted(tail_cot, "ctx", -1)
    whole = lax.dynamic_update_slice(cat, (end + incoming).astype(BF16), (length - PAD, width))
    return ring_scatter((cat, whole), weight_cat, held)


def solution(mesh):
    placed = (
        P(("ctx", "tp"), None),
        P(("ctx", "tp"), None),
        P(None, None, "tp"),
        P(),
        P(None, "tp"),
        P(None, "tp"),
        P(),
        P("tp"),
        P("tp"),
        P("tp"),
        P("tp", None),
    )
    return jax.shard_map(
        body, mesh=mesh, in_specs=placed, out_specs=P(("ctx", "tp"), None), check_vma=False
    )
```

profile of v0, /device:TPU:4, one launch (start us, length us, event | category | flops | bytes accessed | tf_op | source)
XLA Modules:
  0.0 239.1 jit_solution(7848494088831128521)
XLA Ops:
  8.8 3.5 %fusion.1.weight = bf16[4096,896]{1,0:T(8,128)(2,1)} fusion(bf16[4096,2]{1,0:T(8,128)(2,1)S(1)} %copy.12, bf16[4096,256]{1,0:T(8,128)(2,1)S(1)} %copy-done.34, bf16[4096,256]{1,0:T(8,128)(2,1)S(1)} %get-tuple-element.70, bf16[4096,256]{1,0:T(8,128)(2,1)S(1)} %get-tuple-element.69), kind=kLoop, calls=%fused_computation.2 | loop fusion | flops 36700160 | bytes 13647872 | tf_op jit(solution)/shard_map/concatenate | solution.py:405
  12.4 3.8 %collective-permute-done.3 = bf16[48,4096]{1,0:T(8,128)(2,1)} collective-permute-done((bf16[48,4096]{1,0:T(8,128)(2,1)}, bf16[48,4096]{1,0:T(8,128)(2,1)}, u32[]{:S(2)}, u32[]{:S(2)}) %collective-permute-start.3) | collective-permute-done | bytes 393248 | tf_op jit(solution)/shard_map/ppermute | solution.py:279
  16.2 8.4 %collective-permute-done = bf16[48,4096]{1,0:T(8,128)(2,1)} collective-permute-done((bf16[48,4096]{1,0:T(8,128)(2,1)S(1)}, bf16[48,4096]{1,0:T(8,128)(2,1)}, u32[]{:S(2)}, u32[]{:S(2)}) %collective-permute-start) | collective-permute-done | bytes 393248 | tf_op jit(solution)/shard_map/ppermute | solution.py:279
  24.6 5.5 %fusion.48 = bf16[192,896]{1,0:T(8,128)(2,1)S(1)} fusion(bf16[4096,896]{1,0:T(8,128)(2,1)} %fusion.1.weight, bf16[48,4096]{1,0:T(8,128)(2,1)} %collective-permute-done.21, bf16[48,4096]{1,0:T(8,128)(2,1)} %collective-permute-done.20, bf16[96,4096]{1,0:T(8,128)(2,1)} %param.11), kind=kOutput, calls=%fused_computation.51 | convolution fusion | flops 1414176768 | bytes 9256960 | tf_op jit(solution)/shard_map/dot_general | solution.py:28
  30.4 9.9 %collective-permute-done.1 = bf16[48,4096]{1,0:T(8,128)(2,1)S(1)} collective-permute-done((bf16[48,4096]{1,0:T(8,128)(2,1)}, bf16[48,4096]{1,0:T(8,128)(2,1)S(1)}, u32[]{:S(2)}, u32[]{:S(2)}) %collective-permute-start.1) | collective-permute-done | bytes 393248 | tf_op jit(solution)/shard_map/ppermute | solution.py:279
  45.2 9.0 %collective-permute-done.2 = bf16[48,4096]{1,0:T(8,128)(2,1)S(1)} collective-permute-done((bf16[48,4096]{1,0:T(8,128)(2,1)S(1)}, bf16[48,4096]{1,0:T(8,128)(2,1)S(1)}, u32[]{:S(2)}, u32[]{:S(2)}) %collective-permute-start.2) | collective-permute-done | bytes 393248 | tf_op jit(solution)/shard_map/ppermute | solution.py:279
  54.2 6.4 %collective-permute-done.5 = bf16[48,4096]{1,0:T(8,128)(2,1)S(1)} collective-permute-done((bf16[48,4096]{1,0:T(8,128)(2,1)S(1)}, bf16[48,4096]{1,0:T(8,128)(2,1)S(1)}, u32[]{:S(2)}, u32[]{:S(2)}) %collective-permute-start.5) | collective-permute-done | bytes 393248 | tf_op jit(solution)/shard_map/ppermute | solution.py:279
  70.0 12.5 %collective-permute-done.8 = bf16[48,4096]{1,0:T(8,128)(2,1)S(1)} collective-permute-done((bf16[48,4096]{1,0:T(8,128)(2,1)S(1)}, bf16[48,4096]{1,0:T(8,128)(2,1)S(1)}, u32[]{:S(2)}, u32[]{:S(2)}) %collective-permute-start.8) | collective-permute-done | bytes 393248 | tf_op jit(solution)/shard_map/ppermute | solution.py:279
  84.1 4.8 %forward_local.1 = (bf16[768,512]{1,0:T(8,128)(2,1)S(1)}, bf16[768,256]{1,0:T(8,128)(2,1)S(1)}, f32[768,512]{1,0:T(8,128)S(1)}, f32[768,128]{1,0:T(8,128)S(1)}, ...) custom-call(bf16[768,896]{1,0:T(8,128)(2,1)S(1)} %slice_dynamic-upda, ...), custom_call_target="tpu_custom_call" | custom-call | flops 1000 | bytes 1000 | tf_op jit(solution)/shard_map/forward_local/pallas_call | solution.py:428
  90.9 5.4 %collective-permute-done.12 = bf16[48,4096]{1,0:T(8,128)(2,1)S(1)} collective-permute-done((bf16[48,4096]{1,0:T(8,128)(2,1)S(1)}, bf16[48,4096]{1,0:T(8,128)(2,1)S(1)}, u32[]{:S(2)}, u32[]{:S(2)}) %collective-permute-start.12) | collective-permute-done | bytes 393248 | tf_op jit(solution)/shard_map/ppermute | solution.py:279
  106.0 3.5 %forward_carried.1 = (f32[768,256]{1,0:T(8,128)S(1)}, f32[768,256]{1,0:T(8,128)S(1)}, f32[768,256]{1,0:T(8,128)S(1)}, bf16[768,256]{1,0:T(8,128)(2,1)S(1)}, bf16...) custom-call(bf16[768,896]{1,0:T(8,128)(2,1)S(1)} %slice_dynamic-update-slice_fusion.12.proj, ...), custom_call_target="tpu_custom_call" | custom-call | flops 1000 | bytes 1000 | tf_op jit(solution)/shard_map/forward_carried/pallas_call | solution.py:470
  109.6 7.6 %collective-permute-done.16 = bf16[48,4096]{1,0:T(8,128)(2,1)S(1)} collective-permute-done((bf16[48,4096]{1,0:T(8,128)(2,1)S(1)}, bf16[48,4096]{1,0:T(8,128)(2,1)S(1)}, u32[]{:S(2)}, u32[]{:S(2)}) %collective-permute-start.16) | collective-permute-done | bytes 393248 | tf_op jit(solution)/shard_map/ppermute | solution.py:279
  117.2 8.0 %collective-permute-done.18 = bf16[48,4096]{1,0:T(8,128)(2,1)S(1)} collective-permute-done((bf16[48,4096]{1,0:T(8,128)(2,1)S(1)}, bf16[48,4096]{1,0:T(8,128)(2,1)S(1)}, u32[]{:S(2)}, u32[]{:S(2)}) %collective-permute-start.18) | collective-permute-done | bytes 393248 | tf_op jit(solution)/shard_map/ppermute | solution.py:279
  130.1 3.7 %collective-permute-start.35 = (f32[8,768]{1,0:T(8,128)S(1)}, f32[8,768]{1,0:T(8,128)S(1)}, u32[]{:S(2)}, u32[]{:S(2)}) collective-permute-start(f32[8,768]{1,0:T(8,128)S(1)} %add.415.refs_0_), channel_id=1, source_target_pairs={{0,6},{1,7},{2,0},{3,1},{4,2},{5,3},{6,4},{7,5},{8,14},{9,15},{10,... | collective-permute-start | bytes 73736 | tf_op jit(solution)/shard_map/ppermute | solution.py:279
  158.2 5.1 %backward_carried.1 = (bf16[768,896]{1,0:T(8,128)(2,1)S(1)}, f32[8,512]{1,0:T(8,128)S(1)}, f32[8,512]{1,0:T(8,128)}) custom-call(bf16[768,256]{1,0:T(8,128)(2,1)S(1)} %copy-done.20, bf16[768,512]{1,0:T(8,128)(2,1)S(1)} %get-tuple-element.37.act, bf16[768,256]{1,0:T(8,128)(2,1)S(1)} %copy-done.5, f32[768,512]{1,0:T(8,128)S(1)} %copy-done.10, ...), custom_call_target="tpu_custom_call" | custom-call | flops 1000 | bytes 1000 | tf_op jit(solution)/shard_map/backward_carried/pallas_call | solution.py:513
  163.9 4.8 %collective-permute-start.40 = (f32[8,512]{1,0:T(8,128)}, f32[8,512]{1,0:T(8,128)S(1)}, u32[]{:S(2)}, u32[]{:S(2)}) collective-permute-start(f32[8,512]{1,0:T(8,128)} %get-tuple-element.66), channel_id=1, source_target_pairs={{8,0},{16,8},{24,16},{9,1},{17,9},{25,17},{10,2},{18,10},{26,18},{... | collective-permute-start | bytes 49160 | tf_op jit(solution)/shard_map/ppermute | solution.py:290
  171.9 5.0 %product_rows.2 = (bf16[192,4096]{1,0:T(8,128)(2,1)S(1)}, bf16[192,4096]{1,0:T(8,128)(2,1)S(1)}) custom-call(bf16[384,896]{1,0:T(8,128)(2,1)S(1)} %dynamic-slice_dynamic-update-slice_fusion.8.rows, bf16[4096,896]{1,0:T(8,128)(2,1)S(1)} %copy-done.2), custom_call_target="tpu_custom_call" | custom-call | flops 1000 | bytes 1000 | tf_op jit(solution)/shard_map/product_rows/pallas_call | solution.py:348
  177.3 5.1 %product_rows.3 = (bf16[192,4096]{1,0:T(8,128)(2,1)S(1)}, bf16[192,4096]{1,0:T(8,128)(2,1)S(1)}) custom-call(bf16[384,896]{1,0:T(8,128)(2,1)S(1)} %dynamic-slice_dynamic-update-slice_fusion.rows, bf16[4096,896]{1,0:T(8,128)(2,1)S(1)} %copy-done.2), custom_call_target="tpu_custom_call" | custom-call | flops 1000 | bytes 1000 | tf_op jit(solution)/shard_map/product_rows/pallas_call | solution.py:348
  188.1 8.7 %collective-permute-done.42 = bf16[48,4096]{1,0:T(8,128)(2,1)S(1)} collective-permute-done((bf16[48,4096]{1,0:T(8,128)(2,1)S(1)}, bf16[48,4096]{1,0:T(8,128)(2,1)S(1)}, u32[]{:S(2)}, u32[]{:S(2)}) %collective-permute-start.42) | collective-permute-done | bytes 393248 | tf_op jit(solution)/shard_map/ppermute | solution.py:279
  197.3 8.0 %collective-permute-done.45 = bf16[48,4096]{1,0:T(8,128)(2,1)S(1)} collective-permute-done((bf16[48,4096]{1,0:T(8,128)(2,1)S(1)}, bf16[48,4096]{1,0:T(8,128)(2,1)S(1)}, u32[]{:S(2)}, u32[]{:S(2)}) %collective-permute-start.45) | collective-permute-done | bytes 393248 | tf_op jit(solution)/shard_map/ppermute | solution.py:279
  205.7 8.0 %collective-permute-done.43 = bf16[48,4096]{1,0:T(8,128)(2,1)S(1)} collective-permute-done((bf16[48,4096]{1,0:T(8,128)(2,1)S(1)}, bf16[48,4096]{1,0:T(8,128)(2,1)S(1)}, u32[]{:S(2)}, u32[]{:S(2)}) %collective-permute-start.43) | collective-permute-done | bytes 393248 | tf_op jit(solution)/shard_map/ppermute | solution.py:279
  214.1 8.0 %collective-permute-done.46 = bf16[48,4096]{1,0:T(8,128)(2,1)S(1)} collective-permute-done((bf16[48,4096]{1,0:T(8,128)(2,1)S(1)}, bf16[48,4096]{1,0:T(8,128)(2,1)S(1)}, u32[]{:S(2)}, u32[]{:S(2)}) %collective-permute-start.46) | collective-permute-done | bytes 393248 | tf_op jit(solution)/shard_map/ppermute | solution.py:279
  222.5 8.0 %collective-permute-done.44 = bf16[48,4096]{1,0:T(8,128)(2,1)S(1)} collective-permute-done((bf16[48,4096]{1,0:T(8,128)(2,1)S(1)}, bf16[48,4096]{1,0:T(8,128)(2,1)S(1)}, u32[]{:S(2)}, u32[]{:S(2)}) %collective-permute-start.44) | collective-permute-done | bytes 393248 | tf_op jit(solution)/shard_map/ppermute | solution.py:279
  230.7 7.4 %collective-permute-done.47 = bf16[48,4096]{1,0:T(8,128)(2,1)S(1)} collective-permute-done((bf16[48,4096]{1,0:T(8,128)(2,1)S(1)}, bf16[48,4096]{1,0:T(8,128)(2,1)S(1)}, u32[]{:S(2)}, u32[]{:S(2)}) %collective-permute-start.47) | collective-permute-done | bytes 393248 | tf_op jit(solution)/shard_map/ppermute | solution.py:279
  (247 shorter events, 78.2 us)
Async XLA Ops:
  3.7 21.0 %collective-permute-start.21 = (bf16[48,4096]{1,0:T(8,128)(2,1)}, bf16[48,4096]{1,0:T(8,128)(2,1)}, u32[]{:S(2)}, u32[]{:S(2)}) collective-permute-start(bf16[48,4096]{1,0:T(8,128)(2,1)} %get-tuple-element.74), channel_id=1, source_target_pairs={{0,1},{1,0},{2,3},{3,2},{4,5},{5,4},{6,7},{7,6},{8,9},{9,8},{10,11... | collective-permute-start | bytes 1179656 | tf_op jit(solution)/shard_map/ppermute | solution.py:284
  3.7 21.0 %collective-permute-start = (bf16[48,4096]{1,0:T(8,128)(2,1)S(1)}, bf16[48,4096]{1,0:T(8,128)(2,1)}, u32[]{:S(2)}, u32[]{:S(2)}) collective-permute-start(bf16[48,4096]{1,0:T(8,128)(2,1)S(1)} %get-tuple-element.73), channel_id=1, source_target_pairs={{0,2},{1,3},{2,4},{3,5},{4,6},{5,7},{6,0},{7,1},{8,10},{9,11},{10,... | collective-permute-start | bytes 1179656 | tf_op jit(solution)/shard_map/ppermute | solution.py:279
  5.2 19.4 %collective-permute-start.20 = (bf16[48,4096]{1,0:T(8,128)(2,1)S(1)}, bf16[48,4096]{1,0:T(8,128)(2,1)}, u32[]{:S(2)}, u32[]{:S(2)}) collective-permute-start(bf16[48,4096]{1,0:T(8,128)(2,1)S(1)} %get-tuple-element.73), channel_id=1, source_target_pairs={{0,1},{1,0},{2,3},{3,2},{4,5},{5,4},{6,7},{7,6},{8,9},{9,8},{10,11... | collective-permute-start | bytes 1179656 | tf_op jit(solution)/shard_map/ppermute | solution.py:284
  16.2 24.1 %collective-permute-start.4 = (bf16[48,4096]{1,0:T(8,128)(2,1)}, bf16[48,4096]{1,0:T(8,128)(2,1)S(1)}, u32[]{:S(2)}, u32[]{:S(2)}) collective-permute-start(bf16[48,4096]{1,0:T(8,128)(2,1)} %collective-permute-done.3), channel_id=1, source_target_pairs={{0,2},{1,3},{2,4},{3,5},{4,6},{5,7},{6,0},{7,1},{8,10},{9,11},{10,... | collective-permute-start | bytes 1179656 | tf_op jit(solution)/shard_map/ppermute | solution.py:279
  16.2 25.4 %collective-permute-start.23 = (bf16[48,4096]{1,0:T(8,128)(2,1)}, bf16[48,4096]{1,0:T(8,128)(2,1)S(1)}, u32[]{:S(2)}, u32[]{:S(2)}) collective-permute-start(bf16[48,4096]{1,0:T(8,128)(2,1)} %collective-permute-done.3), channel_id=1, source_target_pairs={{0,1},{1,0},{2,3},{3,2},{4,5},{5,4},{6,7},{7,6},{8,9},{9,8},{10,11... | collective-permute-start | bytes 1179656 | tf_op jit(solution)/shard_map/ppermute | solution.py:284
  24.6 17.0 %collective-permute-start.22 = (bf16[48,4096]{1,0:T(8,128)(2,1)}, bf16[48,4096]{1,0:T(8,128)(2,1)S(1)}, u32[]{:S(2)}, u32[]{:S(2)}) collective-permute-start(bf16[48,4096]{1,0:T(8,128)(2,1)} %collective-permute-done), channel_id=1, source_target_pairs={{0,1},{1,0},{2,3},{3,2},{4,5},{5,4},{6,7},{7,6},{8,9},{9,8},{10,11... | collective-permute-start | bytes 1179656 | tf_op jit(solution)/shard_map/ppermute | solution.py:284
  40.3 20.3 %collective-permute-start.5 = (bf16[48,4096]{1,0:T(8,128)(2,1)S(1)}, bf16[48,4096]{1,0:T(8,128)(2,1)S(1)}, u32[]{:S(2)}, u32[]{:S(2)}) collective-permute-start(bf16[48,4096]{1,0:T(8,128)(2,1)S(1)} %collective-permute-done.4), channel_id=1, source_target_pairs={{0,2},{1,3},{2,4},{3,5},{4,6},{5,7},{6,0},{7,1},{8,10},{9,11},{10,... | collective-permute-start | bytes 1179656 | tf_op jit(solution)/shard_map/ppermute | solution.py:279
  44.6 16.7 %collective-permute-start.25 = (bf16[48,4096]{1,0:T(8,128)(2,1)S(1)}, bf16[48,4096]{1,0:T(8,128)(2,1)S(1)}, u32[]{:S(2)}, u32[]{:S(2)}) collective-permute-start(bf16[48,4096]{1,0:T(8,128)(2,1)S(1)} %collective-permute-done.4), channel_id=1, source_target_pairs={{0,1},{1,0},{2,3},{3,2},{4,5},{5,4},{6,7},{7,6},{8,9},{9,8},{10,11... | collective-permute-start | bytes 1179656 | tf_op jit(solution)/shard_map/ppermute | solution.py:284
  44.7 16.6 %collective-permute-start.24 = (bf16[48,4096]{1,0:T(8,128)(2,1)S(1)}, bf16[48,4096]{1,0:T(8,128)(2,1)S(1)}, u32[]{:S(2)}, u32[]{:S(2)}) collective-permute-start(bf16[48,4096]{1,0:T(8,128)(2,1)S(1)} %collective-permute-done.1), channel_id=1, source_target_pairs={{0,1},{1,0},{2,3},{3,2},{4,5},{5,4},{6,7},{7,6},{8,9},{9,8},{10,11... | collective-permute-start | bytes 1179656 | tf_op jit(solution)/shard_map/ppermute | solution.py:284
  60.7 21.8 %collective-permute-start.7 = (bf16[48,4096]{1,0:T(8,128)(2,1)S(1)}, bf16[48,4096]{1,0:T(8,128)(2,1)S(1)}, u32[]{:S(2)}, u32[]{:S(2)}) collective-permute-start(bf16[48,4096]{1,0:T(8,128)(2,1)S(1)} %get-tuple-element.72), channel_id=1, source_target_pairs={{0,1},{1,0},{2,3},{3,2},{4,5},{5,4},{6,7},{7,6},{8,9},{9,8},{10,11... | collective-permute-start | bytes 1179656 | tf_op jit(solution)/shard_map/ppermute | solution.py:284
  60.8 22.8 %collective-permute-start.9 = (bf16[48,4096]{1,0:T(8,128)(2,1)S(1)}, bf16[48,4096]{1,0:T(8,128)(2,1)S(1)}, u32[]{:S(2)}, u32[]{:S(2)}) collective-permute-start(bf16[48,4096]{1,0:T(8,128)(2,1)S(1)} %get-tuple-element.72), channel_id=1, source_target_pairs={{0,2},{1,3},{2,4},{3,5},{4,6},{5,7},{6,0},{7,1},{8,10},{9,11},{10,... | collective-permute-start | bytes 1179656 | tf_op jit(solution)/shard_map/ppermute | solution.py:279
  60.8 21.7 %collective-permute-start.6 = (bf16[48,4096]{1,0:T(8,128)(2,1)S(1)}, bf16[48,4096]{1,0:T(8,128)(2,1)S(1)}, u32[]{:S(2)}, u32[]{:S(2)}) collective-permute-start(bf16[48,4096]{1,0:T(8,128)(2,1)S(1)} %get-tuple-element.71), channel_id=1, source_target_pairs={{0,1},{1,0},{2,3},{3,2},{4,5},{5,4},{6,7},{7,6},{8,9},{9,8},{10,11... | collective-permute-start | bytes 1179656 | tf_op jit(solution)/shard_map/ppermute | solution.py:284
  61.3 21.2 %collective-permute-start.8 = (bf16[48,4096]{1,0:T(8,128)(2,1)S(1)}, bf16[48,4096]{1,0:T(8,128)(2,1)S(1)}, u32[]{:S(2)}, u32[]{:S(2)}) collective-permute-start(bf16[48,4096]{1,0:T(8,128)(2,1)S(1)} %get-tuple-element.71), channel_id=1, source_target_pairs={{0,2},{1,3},{2,4},{3,5},{4,6},{5,7},{6,0},{7,1},{8,10},{9,11},{10,... | collective-permute-start | bytes 1179656 | tf_op jit(solution)/shard_map/ppermute | solution.py:279
  66.6 17.4 %collective-permute-start.28 = (bf16[8,512]{1,0:T(8,128)(2,1)S(1)}, bf16[8,512]{1,0:T(8,128)(2,1)S(1)}, u32[]{:S(2)}, u32[]{:S(2)}) collective-permute-start(bf16[8,512]{1,0:T(8,128)(2,1)S(1)} %slice.231), channel_id=1, source_target_pairs={{0,8},{8,16},{16,24},{1,9},{9,17},{17,25},{2,10},{10,18},{18,26},{... | collective-permute-start | bytes 24584 | tf_op jit(solution)/shard_map/ppermute | solution.py:290
  83.5 15.9 %collective-permute-start.10 = (bf16[48,4096]{1,0:T(8,128)(2,1)S(1)}, bf16[48,4096]{1,0:T(8,128)(2,1)S(1)}, u32[]{:S(2)}, u32[]{:S(2)}) collective-permute-start(bf16[48,4096]{1,0:T(8,128)(2,1)S(1)} %collective-permute-done.8), channel_id=1, source_target_pairs={{0,1},{1,0},{2,3},{3,2},{4,5},{5,4},{6,7},{7,6},{8,9},{9,8},{10,11... | collective-permute-start | bytes 1179656 | tf_op jit(solution)/shard_map/ppermute | solution.py:284
  84.1 19.3 %collective-permute-start.13 = (bf16[48,4096]{1,0:T(8,128)(2,1)S(1)}, bf16[48,4096]{1,0:T(8,128)(2,1)S(1)}, u32[]{:S(2)}, u32[]{:S(2)}) collective-permute-start(bf16[48,4096]{1,0:T(8,128)(2,1)S(1)} %collective-permute-done.9), channel_id=1, source_target_pairs={{0,2},{1,3},{2,4},{3,5},{4,6},{5,7},{6,0},{7,1},{8,10},{9,11},{10,... | collective-permute-start | bytes 1179656 | tf_op jit(solution)/shard_map/ppermute | solution.py:279
  99.4 25.8 %collective-permute-start.14 = (bf16[48,4096]{1,0:T(8,128)(2,1)S(1)}, bf16[48,4096]{1,0:T(8,128)(2,1)S(1)}, u32[]{:S(2)}, u32[]{:S(2)}) collective-permute-start(bf16[48,4096]{1,0:T(8,128)(2,1)S(1)} %collective-permute-done.12), channel_id=1, source_target_pairs={{0,1},{1,0},{2,3},{3,2},{4,5},{5,4},{6,7},{7,6},{8,9},{9,8},{10,11... | collective-permute-start | bytes 1179656 | tf_op jit(solution)/shard_map/ppermute | solution.py:284
  103.4 21.8 %collective-permute-start.15 = (bf16[48,4096]{1,0:T(8,128)(2,1)S(1)}, bf16[48,4096]{1,0:T(8,128)(2,1)S(1)}, u32[]{:S(2)}, u32[]{:S(2)}) collective-permute-start(bf16[48,4096]{1,0:T(8,128)(2,1)S(1)} %collective-permute-done.13), channel_id=1, source_target_pairs={{0,1},{1,0},{2,3},{3,2},{4,5},{5,4},{6,7},{7,6},{8,9},{9,8},{10,11... | collective-permute-start | bytes 1179656 | tf_op jit(solution)/shard_map/ppermute | solution.py:284
  103.5 21.7 %collective-permute-start.18 = (bf16[48,4096]{1,0:T(8,128)(2,1)S(1)}, bf16[48,4096]{1,0:T(8,128)(2,1)S(1)}, u32[]{:S(2)}, u32[]{:S(2)}) collective-permute-start(bf16[48,4096]{1,0:T(8,128)(2,1)S(1)} %collective-permute-done.13), channel_id=1, source_target_pairs={{0,2},{1,3},{2,4},{3,5},{4,6},{5,7},{6,0},{7,1},{8,10},{9,11},{10,... | collective-permute-start | bytes 1179656 | tf_op jit(solution)/shard_map/ppermute | solution.py:279
  186.0 19.2 %collective-permute-start.45 = (bf16[48,4096]{1,0:T(8,128)(2,1)S(1)}, bf16[48,4096]{1,0:T(8,128)(2,1)S(1)}, u32[]{:S(2)}, u32[]{:S(2)}) collective-permute-start(bf16[48,4096]{1,0:T(8,128)(2,1)S(1)} %add_convert_fusion.7), channel_id=1, source_target_pairs={{0,2},{1,3},{2,4},{3,5},{4,6},{5,7},{6,0},{7,1},{8,10},{9,11},{10,... | collective-permute-start | bytes 1179656 | tf_op jit(solution)/shard_map/ppermute | solution.py:279
  197.0 16.7 %collective-permute-start.43 = (bf16[48,4096]{1,0:T(8,128)(2,1)S(1)}, bf16[48,4096]{1,0:T(8,128)(2,1)S(1)}, u32[]{:S(2)}, u32[]{:S(2)}) collective-permute-start(bf16[48,4096]{1,0:T(8,128)(2,1)S(1)} %add_convert_fusion.5), channel_id=1, source_target_pairs={{0,2},{1,3},{2,4},{3,5},{4,6},{5,7},{6,0},{7,1},{8,10},{9,11},{10,... | collective-permute-start | bytes 1179656 | tf_op jit(solution)/shard_map/ppermute | solution.py:279
  205.4 16.7 %collective-permute-start.46 = (bf16[48,4096]{1,0:T(8,128)(2,1)S(1)}, bf16[48,4096]{1,0:T(8,128)(2,1)S(1)}, u32[]{:S(2)}, u32[]{:S(2)}) collective-permute-start(bf16[48,4096]{1,0:T(8,128)(2,1)S(1)} %add_convert_fusion.2), channel_id=1, source_target_pairs={{0,2},{1,3},{2,4},{3,5},{4,6},{5,7},{6,0},{7,1},{8,10},{9,11},{10,... | collective-permute-start | bytes 1179656 | tf_op jit(solution)/shard_map/ppermute | solution.py:279
  213.8 16.7 %collective-permute-start.44 = (bf16[48,4096]{1,0:T(8,128)(2,1)S(1)}, bf16[48,4096]{1,0:T(8,128)(2,1)S(1)}, u32[]{:S(2)}, u32[]{:S(2)}) collective-permute-start(bf16[48,4096]{1,0:T(8,128)(2,1)S(1)} %add_convert_fusion.4), channel_id=1, source_target_pairs={{0,2},{1,3},{2,4},{3,5},{4,6},{5,7},{6,0},{7,1},{8,10},{9,11},{10,... | collective-permute-start | bytes 1179656 | tf_op jit(solution)/shard_map/ppermute | solution.py:279
  222.2 15.8 %collective-permute-start.47 = (bf16[48,4096]{1,0:T(8,128)(2,1)S(1)}, bf16[48,4096]{1,0:T(8,128)(2,1)S(1)}, u32[]{:S(2)}, u32[]{:S(2)}) collective-permute-start(bf16[48,4096]{1,0:T(8,128)(2,1)S(1)} %add_convert_fusion.1), channel_id=1, source_target_pairs={{0,2},{1,3},{2,4},{3,5},{4,6},{5,7},{6,0},{7,1},{8,10},{9,11},{10,... | collective-permute-start | bytes 1179656 | tf_op jit(solution)/shard_map/ppermute | solution.py:279
  (65 other events, 484.5 us)
where the time goes:
time: 240 us; the launch traced here: 239 us
  waiting for transfers between devices  128 us (53%)
  starting transfers between devices  31.4 us (13%)
  Pallas kernels  30.3 us (13%)
  local copies, waits for them, and re-layouts  24 us (10%)
  matrix products  16.9 us (7%)
  other arithmetic  7.25 us (3%)
    ppermute x27, waiting for transfers between devices, turned(): lax.ppermute(value, axis, [(i, (i + by) % length) for i in range(length)])  126 us
    ppermute x27, starting transfers between devices, turned(): lax.ppermute(value, axis, [(i, (i + by) % length) for i in range(length)])  19.7 us
    unnamed x98, local copies, waits for them, and re-layouts  18.6 us
    dot_general x10, matrix products, dot(): lax.dot_general(a, b, (((over[0],), (over[1],)), ((), ())), precision=pre...  16.9 us
    pallas_call x2, Pallas kernels, multiply_rows(): pl.pallas_call(product_rows, grid=(depth // block,), in_specs=[pl.BlockSp...  10.1 us
    ppermute x2, starting transfers between devices, shifted(): return lax.ppermute(value, axis, pairs)  8.21 us
    pallas_call x1, Pallas kernels, body(): pl.pallas_call(partial(backward_carried, heads, block), out_shape=[shape(...  5.14 us
  transfers between devices with their start and end apart: 48, of which 23 were waited for; matrix products, arithmetic and copies ran while one was open for 11% of the time, Pallas kernels for 9%

commit v1 on v0

--- a/solution.py
+++ b/solution.py
@@ -40,14 +40,24 @@
     return slice(h * HEAD_DIM, (h + 1) * HEAD_DIM)
 
 
+def columns(ref, *widths):
+    views = []
+    first = 0
+    for size in widths:
+        views.append(ref.at[:, first : first + size])
+        first = first + size
+    return views
+
+
 def forward_local(
     heads, block, proj, tail, kern, bias, rate,
-    act_out, scaled_out, slope_out, step_out, run_out, sig_out, decay_out, table_out, diag_out, states_out,
-    own_out, ext,
+    saved_out, factors_out, diag_out, states_out, own_out, ext,
 ):
     length = proj.shape[0]
     width = heads * HEAD_DIM
     conv_width = width + 2 * STATE
+    act_out, scaled_out, decay_out, table_out = columns(saved_out, conv_width, width, width, width)
+    slope_out, step_out, run_out, sig_out = columns(factors_out, conv_width, LANES, LANES, LANES)
     ext[0:PAD, :] = tail[...].astype(F32)
     ext[PAD:, :] = proj[:, width : width + conv_width].astype(F32)
     causal = triangle(block, lambda i, j: i >= j)
@@ -94,12 +104,17 @@
 
 
 def forward_carried(
-    heads, block, proj, act, run, diag, states, weights, *refs,
+    heads, block, proj, saved, factors, diag, states, weights, *refs,
 ):
-    received = refs[:-6]
-    gated_out, silu_out, slope_out, carried_out, states_out, sums_out = refs[-6:]
+    received = refs[:-3]
+    gates_out, sent_out, sums_out = refs[-3:]
     length = proj.shape[0]
     width = heads * HEAD_DIM
+    conv_width = width + 2 * STATE
+    (act,) = columns(saved, conv_width)
+    _, _, run = columns(factors, conv_width, LANES, LANES)
+    gated_out, silu_out, slope_out = columns(gates_out, width, width, width)
+    carried_out, states_out = columns(sent_out, width, width)
     entering = []
     for h in range(heads):
         total = jnp.zeros((HEAD_DIM, STATE), F32)
@@ -118,7 +133,7 @@
             at = k * heads + h
             here = slice(at * HEAD_DIM, (at + 1) * HEAD_DIM)
             state = states[here, :] + reach[:, h : h + 1] * entering[h]
-            states_out[here, :] = state.astype(BF16)
+            states_out[rows, head(h)] = state.astype(BF16)
             carried = grow[:, h : h + 1] * dot(c_rows, state, (1, 1), EXACT)
             carried_out[rows, head(h)] = carried.astype(BF16)
             out = diag[rows, head(h)] + carried
@@ -133,18 +148,24 @@
         sums_out[:, rows] = dot(ones, gated * gated, (1, 1), EXACT)
 
 
-def token_sums(local, gain, gated, squares, sums_out):
+def token_sums(local, gain, gates, squares, sums_out):
+    (gated,) = columns(gates, local.shape[1])
     ones = jnp.ones((8, local.shape[1]), F32)
     cross = dot(ones, gain[...] * local[...] * gated[...], (1, 1), EXACT)
     upper = lax.broadcasted_iota(jnp.int32, cross.shape, 0) < 4
     sums_out[...] = jnp.where(upper, squares[...], cross)
 
 
-def backward_gate(heads, block, total_width, local, gain, gated, silu, slope, act, run, *refs):
-    parts = refs[:-5]
-    dgate_out, cot_out, grown_out, blocks_out, own_out = refs[-5:]
+def backward_gate(heads, block, total_width, local, gain, gates, saved, factors, *refs):
+    parts = refs[:-3]
+    cots_out, blocks_out, own_out = refs[-3:]
     length = local.shape[0]
     width = heads * HEAD_DIM
+    conv_width = width + 2 * STATE
+    gated, silu, slope = columns(gates, width, width, width)
+    (act,) = columns(saved, conv_width)
+    _, _, run = columns(factors, conv_width, LANES, LANES)
+    dgate_out, cot_out, grown_out = columns(cots_out, width, width, width)
     pick = lax.broadcasted_iota(jnp.int32, (8, LANES), 0)
     own = [jnp.zeros((HEAD_DIM, STATE), F32) for _ in range(heads)]
     base = jnp.zeros((1, LANES), F32)
@@ -177,11 +198,13 @@
         own_out[head(h), :] = own[h]
 
 
-def backward_local(
-    heads, block, cot, grown, act, scaled, decays, table, states, carried, u_out, dbc_out, decay_out
-):
-    length = cot.shape[0]
+def backward_local(heads, block, cots, saved, sent, near_out):
+    length = cots.shape[0]
     width = heads * HEAD_DIM
+    _, cot, grown = columns(cots, width, width, width)
+    act, scaled, decays, table = columns(saved, width + 2 * STATE, width, width, width)
+    carried, states = columns(sent, width, width)
+    u_out, dbc_out, decay_out = columns(near_out, width, 2 * STATE, LANES)
     before = triangle(block, lambda i, j: i > j)
     upper = triangle(block, lambda i, j: i <= j).astype(BF16)
     lane = lax.broadcasted_iota(jnp.int32, (block, LANES), 1)
@@ -193,14 +216,13 @@
         d_crows = jnp.zeros((block, STATE), F32)
         decay = jnp.zeros((block, LANES), F32)
         for h in range(heads):
-            at = k * heads + h
             g = cot[rows, head(h)]
             weights = table[rows, head(h)]
             inner = dot(g, scaled[rows, head(h)], (1, 1))
             pairs = (decays[rows, head(h)].astype(F32) * inner).astype(BF16)
             mixed = (weights.astype(F32) * inner).astype(BF16)
             d_crows = d_crows + dot(pairs, b_rows)
-            d_crows = d_crows + dot(grown[rows, head(h)], states[at * HEAD_DIM : (at + 1) * HEAD_DIM, :])
+            d_crows = d_crows + dot(grown[rows, head(h)], states[rows, head(h)])
             d_brows = d_brows + dot(pairs, c_rows, (0, 0))
             u_out[rows, head(h)] = dot(weights, g, (0, 0))
             through = (g.astype(F32) * carried[rows, head(h)].astype(F32)).astype(BF16)
@@ -212,14 +234,18 @@
 
 
 def backward_carried(
-    heads, block, dgate, act, scaled, slope, step, run, sig, rate, kern, states, blocks, u, dbc, decay, weights,
-    *refs,
+    heads, block, cots, saved, factors, rate, kern, sent, blocks, near, weights, *refs,
 ):
     received = refs[:-4]
     cat_out, end_out, tail_out, scr = refs[-4:]
-    length = dgate.shape[0]
+    length = cots.shape[0]
     width = heads * HEAD_DIM
     conv_width = width + 2 * STATE
+    (dgate,) = columns(cots, width)
+    act, scaled = columns(saved, conv_width, width)
+    slope, step, run, sig = columns(factors, conv_width, LANES, LANES, LANES)
+    _, states = columns(sent, width, width)
+    u, dbc, decay = columns(near, width, 2 * STATE, LANES)
     strict = triangle(block, lambda i, j: i > j).astype(BF16)
     lane = lax.broadcasted_iota(jnp.int32, (block, LANES), 1)
     scr[0:PAD, :] = jnp.zeros((PAD, conv_width), F32)
@@ -251,7 +277,7 @@
             d_brows = d_brows + dot((shrink[:, h : h + 1] * moved).astype(BF16), cot_state)
             kept = whole[:, h : h + 1] * leaving[h]
             constant = jnp.sum(
-                jnp.sum(kept * states[here, :].astype(F32), axis=1, keepdims=True), axis=0, keepdims=True
+                jnp.sum(kept * states[rows, head(h)].astype(F32), axis=1, keepdims=True), axis=0, keepdims=True
             )
             spread = dot(strict, (moved * past).astype(BF16))
             d_decay = jnp.sum(spread, axis=1, keepdims=True) + constant + decay[rows, h : h + 1]
@@ -424,18 +450,13 @@
         jnp.zeros((length, width), F32),
     )
 
-    tail = shifted(proj[length - PAD :, width : width + conv_width], "ctx", 1)
-    act, scaled, slope, step, run, sig, decays, table, diag, states, own = pl.pallas_call(
+    tail = after(proj[length - PAD :, width : width + conv_width], grads_in[0][1])
+    tail = after(shifted(tail, "ctx", 1), grads_in[0][0])
+    saved, factors, diag, states, own = pl.pallas_call(
         partial(forward_local, heads, block),
         out_shape=[
-            shape(length, conv_width, dtype=BF16),
-            shape(length, width, dtype=BF16),
-            shape(length, conv_width),
-            shape(length, LANES),
-            shape(length, LANES),
-            shape(length, LANES),
-            shape(length, heads * block, dtype=BF16),
-            shape(length, heads * block, dtype=BF16),
+            shape(length, conv_width + 3 * width, dtype=BF16),
+            shape(length, conv_width + 3 * LANES),
             shape(length, width),
             shape(count * heads * HEAD_DIM, STATE),
             shape(heads * HEAD_DIM, STATE),
@@ -445,11 +466,12 @@
         **PARAMS,
     )(proj, tail, kern, bias, rate)
 
+    run = factors[:, conv_width + LANES : conv_width + 2 * LANES]
     ends = run.reshape(count, block, LANES)[:, block - 1, :heads]
     total_log = jnp.sum(ends, axis=0)
     message = jnp.concatenate([own, jnp.broadcast_to(jnp.pad(total_log, (0, LANES - heads)), (8, LANES))], axis=0)
     second = grads_in[min(1, len(grads_in) - 1)]
-    message = after(message, second[0])
+    message = after(message, second[1])
     received = [turned(message, "ctx", by) for by in range(1, shards)]
     logs = [part[heads * HEAD_DIM, :heads] for part in received]
     entering_weights = []
@@ -467,48 +489,43 @@
         flat = jnp.concatenate(parts)
         return jnp.broadcast_to(flat[:, None], (flat.shape[0], LANES))
 
-    gated, silu, gate_slope, carried, full_states, squares = pl.pallas_call(
+    gates, sent, squares = pl.pallas_call(
         partial(forward_carried, heads, block),
         out_shape=[
-            shape(length, width),
-            shape(length, width),
-            shape(length, width),
-            shape(length, width, dtype=BF16),
-            shape(count * heads * HEAD_DIM, STATE, dtype=BF16),
+            shape(length, 3 * width),
+            shape(length, 2 * width, dtype=BF16),
             shape(8, length),
         ],
         name="forward_carried",
         **PARAMS,
-    )(proj, act, run, diag, states, after(spread(entering_weights), second[1]), *received)
+    )(proj, saved, factors, diag, states, after(spread(entering_weights), second[0]), *received)
 
     sums = pl.pallas_call(token_sums, out_shape=shape(8, length), name="token_sums", **PARAMS)(
-        local, gain, gated, squares
+        local, gain, gates, squares
     )
 
     sums = sums + paired(sums, 1)
     parts = [sums] + [turned(sums, "tp", by) for by in range(2, members, 2)]
 
-    dgate, cot, grown, blocks, own_cot = pl.pallas_call(
+    cots, blocks, own_cot = pl.pallas_call(
         partial(backward_gate, heads, block, width * members),
         out_shape=[
-            shape(length, width, dtype=BF16),
-            shape(length, width, dtype=BF16),
-            shape(length, width, dtype=BF16),
+            shape(length, 3 * width, dtype=BF16),
             shape(count * heads * HEAD_DIM, STATE),
             shape(heads * HEAD_DIM, STATE),
         ],
         name="backward_gate",
         **PARAMS,
-    )(local, gain, gated, silu, gate_slope, act, run, *parts)
+    )(local, gain, gates, saved, factors, *parts)
 
     returned = [turned(own_cot, "ctx", -by) for by in range(1, shards)]
 
-    u, dbc, decay = pl.pallas_call(
+    near = pl.pallas_call(
         partial(backward_local, heads, block),
-        out_shape=[shape(length, width), shape(length, 2 * STATE), shape(length, LANES)],
+        out_shape=shape(length, width + 2 * STATE + LANES),
         name="backward_local",
         **PARAMS,
-    )(cot, grown, act, scaled, decays, table, full_states, carried)
+    )(cots, saved, sent)
 
     cat, end, tail_cot = pl.pallas_call(
         partial(backward_carried, heads, block),
@@ -521,7 +538,7 @@
         name="backward_carried",
         **PARAMS,
     )(
-        dgate, act, scaled, slope, step, run, sig, rate, kern, full_states, blocks, u, dbc, decay,
+        cots, saved, factors, rate, kern, sent, blocks, near,
         spread(leaving_weights), *returned,
     )
 

time: 240 us -> 227 us (0.946)
  local copies, waits for them, and re-layouts: 24 us -> 13.6 us
    unnamed x98 -> x64, local copies, waits for them, and re-layouts: 18.6 us -> 8.19 us
  transfers between devices with their start and end apart: 48 -> 48, of which waited for: 23 -> 25; matrix products, arithmetic and copies ran while one was open for 11% -> 11% of each run, Pallas kernels for 9% -> 9%
where the time goes in v1:
time: 227 us; the launch traced here: 226 us
  waiting for transfers between devices  128 us (56%)
  Pallas kernels  30.3 us (13%)
  starting transfers between devices  29.6 us (13%)
  matrix products  16.9 us (7%)
  local copies, waits for them, and re-layouts  13.6 us (6%)
  other arithmetic  7.05 us (3%)
    ppermute x27, waiting for transfers between devices, turned(): lax.ppermute(value, axis, [(i, (i + by) % length) for i in range(length)])  126 us
    ppermute x27, starting transfers between devices, turned(): lax.ppermute(value, axis, [(i, (i + by) % length) for i in range(length)])  18.8 us
    dot_general x10, matrix products, dot(): lax.dot_general(a, b, (((over[0],), (over[1],)), ((), ())), precision=pre...  16.9 us
    pallas_call x2, Pallas kernels, multiply_rows(): pl.pallas_call(product_rows, grid=(depth // block,), in_specs=[pl.BlockSp...  10.1 us
    unnamed x64, local copies, waits for them, and re-layouts  8.19 us
    ppermute x2, starting transfers between devices, shifted(): return lax.ppermute(value, axis, pairs)  7.71 us
    pallas_call x1, Pallas kernels, body(): pl.pallas_call(partial(backward_carried, heads, block), out_shape=[shape(...  5.12 us
    pallas_call x1, Pallas kernels, body(): pl.pallas_call(partial(forward_local, heads, block), out_shape=[shape(len...  4.79 us
  transfers between devices with their start and end apart: 48, of which 25 were waited for; matrix products, arithmetic and copies ran while one was open for 11% of the time, Pallas kernels for 9%

profile of v1, /device:TPU:4, one launch (start us, length us, event | category | flops | bytes accessed | tf_op | source)
XLA Modules:
  0.0 226.4 jit_solution(4155250200959845472)
XLA Ops:
  12.3 3.9 %collective-permute-done.3 = bf16[48,4096]{1,0:T(8,128)(2,1)} collective-permute-done((bf16[48,4096]{1,0:T(8,128)(2,1)}, bf16[48,4096]{1,0:T(8,128)(2,1)}, u32[]{:S(2)}, u32[]{:S(2)}) %collective-permute-start.3) | collective-permute-done | bytes 393248 | tf_op jit(solution)/shard_map/ppermute | solution.py:305
  16.2 8.4 %collective-permute-done = bf16[48,4096]{1,0:T(8,128)(2,1)} collective-permute-done((bf16[48,4096]{1,0:T(8,128)(2,1)S(1)}, bf16[48,4096]{1,0:T(8,128)(2,1)}, u32[]{:S(2)}, u32[]{:S(2)}) %collective-permute-start) | collective-permute-done | bytes 393248 | tf_op jit(solution)/shard_map/ppermute | solution.py:305
  24.6 5.5 %fusion.48 = bf16[192,896]{1,0:T(8,128)(2,1)S(1)} fusion(bf16[4096,896]{1,0:T(8,128)(2,1)} %fusion.1.weight, bf16[48,4096]{1,0:T(8,128)(2,1)} %collective-permute-done.21, bf16[48,4096]{1,0:T(8,128)(2,1)} %collective-permute-done.20, bf16[96,4096]{1,0:T(8,128)(2,1)} %param.11), kind=kOutput, calls=%fused_computation.51 | convolution fusion | flops 1414176768 | bytes 9256960 | tf_op jit(solution)/shard_map/dot_general | solution.py:28
  30.4 9.9 %collective-permute-done.1 = bf16[48,4096]{1,0:T(8,128)(2,1)S(1)} collective-permute-done((bf16[48,4096]{1,0:T(8,128)(2,1)}, bf16[48,4096]{1,0:T(8,128)(2,1)S(1)}, u32[]{:S(2)}, u32[]{:S(2)}) %collective-permute-start.1) | collective-permute-done | bytes 393248 | tf_op jit(solution)/shard_map/ppermute | solution.py:305
  45.2 9.0 %collective-permute-done.2 = bf16[48,4096]{1,0:T(8,128)(2,1)S(1)} collective-permute-done((bf16[48,4096]{1,0:T(8,128)(2,1)S(1)}, bf16[48,4096]{1,0:T(8,128)(2,1)S(1)}, u32[]{:S(2)}, u32[]{:S(2)}) %collective-permute-start.2) | collective-permute-done | bytes 393248 | tf_op jit(solution)/shard_map/ppermute | solution.py:305
  54.2 6.4 %collective-permute-done.5 = bf16[48,4096]{1,0:T(8,128)(2,1)S(1)} collective-permute-done((bf16[48,4096]{1,0:T(8,128)(2,1)S(1)}, bf16[48,4096]{1,0:T(8,128)(2,1)S(1)}, u32[]{:S(2)}, u32[]{:S(2)}) %collective-permute-start.5) | collective-permute-done | bytes 393248 | tf_op jit(solution)/shard_map/ppermute | solution.py:305
  66.6 7.9 %collective-permute-done.9 = bf16[48,4096]{1,0:T(8,128)(2,1)S(1)} collective-permute-done((bf16[48,4096]{1,0:T(8,128)(2,1)S(1)}, bf16[48,4096]{1,0:T(8,128)(2,1)S(1)}, u32[]{:S(2)}, u32[]{:S(2)}) %collective-permute-start.9) | collective-permute-done | bytes 393248 | tf_op jit(solution)/shard_map/ppermute | solution.py:305
  82.6 4.8 %forward_local.1 = (bf16[768,1280]{1,0:T(8,128)(2,1)S(1)}, f32[768,896]{1,0:T(8,128)S(1)}, f32[768,256]{1,0:T(8,128)S(1)}, f32[1536,128]{1,0:T(8,128)S(1)}, f32[256,128]{1,0:T(8,128)S(1)}) custom-call(bf16[768,896]{1,0:T(8,128)(2,1)S(1)} %slice_dynamic-update-slice_fusion.12.proj, bf16[8,512]{1,0:T(8,128)(2,1)S(1)} %broadcast_add_fusion.tail, ...), custom_call_target="tpu_custom_call" | custom-call | flops 1000 | bytes 1000 | tf_op jit(solution)/shard_map/forward_local/pallas_call | solution.py:455
  87.5 4.4 %collective-permute-done.13 = bf16[48,4096]{1,0:T(8,128)(2,1)S(1)} collective-permute-done((bf16[48,4096]{1,0:T(8,128)(2,1)S(1)}, bf16[48,4096]{1,0:T(8,128)(2,1)S(1)}, u32[]{:S(2)}, u32[]{:S(2)}) %collective-permute-start.13) | collective-permute-done | bytes 393248 | tf_op jit(solution)/shard_map/ppermute | solution.py:305
  95.4 4.4 %collective-permute-done.12 = bf16[48,4096]{1,0:T(8,128)(2,1)S(1)} collective-permute-done((bf16[48,4096]{1,0:T(8,128)(2,1)S(1)}, bf16[48,4096]{1,0:T(8,128)(2,1)S(1)}, u32[]{:S(2)}, u32[]{:S(2)}) %collective-permute-start.12) | collective-permute-done | bytes 393248 | tf_op jit(solution)/shard_map/ppermute | solution.py:305
  101.8 3.5 %forward_carried.1 = (f32[768,768]{1,0:T(8,128)S(1)}, bf16[768,512]{1,0:T(8,128)(2,1)S(1)}, f32[8,768]{1,0:T(8,128)S(1)}) custom-call(bf16[768,896]{1,0:T(8,128)(2,1)S(1)} %slice_dynamic-update-slice_fusion.12.proj, bf16[768,1280]{1,0:T(8,128)(2,1)S(1)} %get-tuple-element.23.saved, f32[768,896]{1,0:T(8,128)S(1)} %get-tuple-element.24.factors, ...), custom_call_target="tpu_custom_call" | custom-call | flops 1000 | bytes 1000 | tf_op jit(solution)/shard_map/forward_carried/pallas_call | solution.py:492
  105.3 8.3 %collective-permute-done.16 = bf16[48,4096]{1,0:T(8,128)(2,1)S(1)} collective-permute-done((bf16[48,4096]{1,0:T(8,128)(2,1)S(1)}, bf16[48,4096]{1,0:T(8,128)(2,1)S(1)}, u32[]{:S(2)}, u32[]{:S(2)}) %collective-permute-start.16) | collective-permute-done | bytes 393248 | tf_op jit(solution)/shard_map/ppermute | solution.py:305
  113.6 8.0 %collective-permute-done.18 = bf16[48,4096]{1,0:T(8,128)(2,1)S(1)} collective-permute-done((bf16[48,4096]{1,0:T(8,128)(2,1)S(1)}, bf16[48,4096]{1,0:T(8,128)(2,1)S(1)}, u32[]{:S(2)}, u32[]{:S(2)}) %collective-permute-start.18) | collective-permute-done | bytes 393248 | tf_op jit(solution)/shard_map/ppermute | solution.py:305
  126.4 3.7 %collective-permute-start.35 = (f32[8,768]{1,0:T(8,128)S(1)}, f32[8,768]{1,0:T(8,128)S(1)}, u32[]{:S(2)}, u32[]{:S(2)}) collective-permute-start(f32[8,768]{1,0:T(8,128)S(1)} %add.441.refs_0_), channel_id=1, source_target_pairs={{0,6},{1,7},{2,0},{3,1},{4,2},{5,3},{6,4},{7,5},{8,14},{9,15},{10,... | collective-permute-start | bytes 73736 | tf_op jit(solution)/shard_map/ppermute | solution.py:305
  146.0 5.1 %backward_carried.1 = (bf16[768,896]{1,0:T(8,128)(2,1)S(1)}, f32[8,512]{1,0:T(8,128)S(1)}, f32[8,512]{1,0:T(8,128)}) custom-call(bf16[768,768]{1,0:T(8,128)(2,1)S(1)} %get-tuple-element.30.cots, bf16[768,1280]{1,0:T(8,128)(2,1)S(1)} %copy-done.5, f32[768,896]{1,0:T(8,128)S(1)} %copy-done.7, f32[1,128]{1,0:T(1,128)S(1)} %get-tuple-element.51.rate, ...), custom_call_target="tpu_custom_call" | custom-call | flops 1000 | bytes 1000 | tf_op jit(solution)/shard_map/backward_carried/pallas_call | solution.py:530
  151.7 4.3 %collective-permute-start.40 = (f32[8,512]{1,0:T(8,128)}, f32[8,512]{1,0:T(8,128)S(1)}, u32[]{:S(2)}, u32[]{:S(2)}) collective-permute-start(f32[8,512]{1,0:T(8,128)} %get-tuple-element.38), channel_id=1, source_target_pairs={{8,0},{16,8},{24,16},{9,1},{17,9},{25,17},{10,2},{18,10},{26,18},{... | collective-permute-start | bytes 49160 | tf_op jit(solution)/shard_map/ppermute | solution.py:316
  159.1 5.0 %product_rows.2 = (bf16[192,4096]{1,0:T(8,128)(2,1)S(1)}, bf16[192,4096]{1,0:T(8,128)(2,1)S(1)}) custom-call(bf16[384,896]{1,0:T(8,128)(2,1)S(1)} %dynamic-slice_dynamic-update-slice_fusion.8.rows, bf16[4096,896]{1,0:T(8,128)(2,1)S(1)} %copy-done.2), custom_call_target="tpu_custom_call" | custom-call | flops 1000 | bytes 1000 | tf_op jit(solution)/shard_map/product_rows/pallas_call | solution.py:374
  164.5 5.1 %product_rows.3 = (bf16[192,4096]{1,0:T(8,128)(2,1)S(1)}, bf16[192,4096]{1,0:T(8,128)(2,1)S(1)}) custom-call(bf16[384,896]{1,0:T(8,128)(2,1)S(1)} %dynamic-slice_dynamic-update-slice_fusion.rows, bf16[4096,896]{1,0:T(8,128)(2,1)S(1)} %copy-done.2), custom_call_target="tpu_custom_call" | custom-call | flops 1000 | bytes 1000 | tf_op jit(solution)/shard_map/product_rows/pallas_call | solution.py:374
  175.4 8.7 %collective-permute-done.42 = bf16[48,4096]{1,0:T(8,128)(2,1)S(1)} collective-permute-done((bf16[48,4096]{1,0:T(8,128)(2,1)S(1)}, bf16[48,4096]{1,0:T(8,128)(2,1)S(1)}, u32[]{:S(2)}, u32[]{:S(2)}) %collective-permute-start.42) | collective-permute-done | bytes 393248 | tf_op jit(solution)/shard_map/ppermute | solution.py:305
  184.5 8.0 %collective-permute-done.45 = bf16[48,4096]{1,0:T(8,128)(2,1)S(1)} collective-permute-done((bf16[48,4096]{1,0:T(8,128)(2,1)S(1)}, bf16[48,4096]{1,0:T(8,128)(2,1)S(1)}, u32[]{:S(2)}, u32[]{:S(2)}) %collective-permute-start.45) | collective-permute-done | bytes 393248 | tf_op jit(solution)/shard_map/ppermute | solution.py:305
  192.9 8.0 %collective-permute-done.43 = bf16[48,4096]{1,0:T(8,128)(2,1)S(1)} collective-permute-done((bf16[48,4096]{1,0:T(8,128)(2,1)S(1)}, bf16[48,4096]{1,0:T(8,128)(2,1)S(1)}, u32[]{:S(2)}, u32[]{:S(2)}) %collective-permute-start.43) | collective-permute-done | bytes 393248 | tf_op jit(solution)/shard_map/ppermute | solution.py:305
  201.3 8.0 %collective-permute-done.46 = bf16[48,4096]{1,0:T(8,128)(2,1)S(1)} collective-permute-done((bf16[48,4096]{1,0:T(8,128)(2,1)S(1)}, bf16[48,4096]{1,0:T(8,128)(2,1)S(1)}, u32[]{:S(2)}, u32[]{:S(2)}) %collective-permute-start.46) | collective-permute-done | bytes 393248 | tf_op jit(solution)/shard_map/ppermute | solution.py:305
  209.8 8.0 %collective-permute-done.44 = bf16[48,4096]{1,0:T(8,128)(2,1)S(1)} collective-permute-done((bf16[48,4096]{1,0:T(8,128)(2,1)S(1)}, bf16[48,4096]{1,0:T(8,128)(2,1)S(1)}, u32[]{:S(2)}, u32[]{:S(2)}) %collective-permute-start.44) | collective-permute-done | bytes 393248 | tf_op jit(solution)/shard_map/ppermute | solution.py:305
  217.9 7.4 %collective-permute-done.47 = bf16[48,4096]{1,0:T(8,128)(2,1)S(1)} collective-permute-done((bf16[48,4096]{1,0:T(8,128)(2,1)S(1)}, bf16[48,4096]{1,0:T(8,128)(2,1)S(1)}, u32[]{:S(2)}, u32[]{:S(2)}) %collective-permute-start.47) | collective-permute-done | bytes 393248 | tf_op jit(solution)/shard_map/ppermute | solution.py:305
  (217 shorter events, 70.0 us)
Async XLA Ops:
  2.1 14.1 %collective-permute-start.3 = (bf16[48,4096]{1,0:T(8,128)(2,1)}, bf16[48,4096]{1,0:T(8,128)(2,1)}, u32[]{:S(2)}, u32[]{:S(2)}) collective-permute-start(bf16[48,4096]{1,0:T(8,128)(2,1)} %get-tuple-element.46), channel_id=1, source_target_pairs={{0,2},{1,3},{2,4},{3,5},{4,6},{5,7},{6,0},{7,1},{8,10},{9,11},{10,... | collective-permute-start | bytes 1179656 | tf_op jit(solution)/shard_map/ppermute | solution.py:305
  3.7 21.0 %collective-permute-start.21 = (bf16[48,4096]{1,0:T(8,128)(2,1)}, bf16[48,4096]{1,0:T(8,128)(2,1)}, u32[]{:S(2)}, u32[]{:S(2)}) collective-permute-start(bf16[48,4096]{1,0:T(8,128)(2,1)} %get-tuple-element.46), channel_id=1, source_target_pairs={{0,1},{1,0},{2,3},{3,2},{4,5},{5,4},{6,7},{7,6},{8,9},{9,8},{10,11... | collective-permute-start | bytes 1179656 | tf_op jit(solution)/shard_map/ppermute | solution.py:310
  3.7 21.0 %collective-permute-start = (bf16[48,4096]{1,0:T(8,128)(2,1)S(1)}, bf16[48,4096]{1,0:T(8,128)(2,1)}, u32[]{:S(2)}, u32[]{:S(2)}) collective-permute-start(bf16[48,4096]{1,0:T(8,128)(2,1)S(1)} %get-tuple-element.45), channel_id=1, source_target_pairs={{0,2},{1,3},{2,4},{3,5},{4,6},{5,7},{6,0},{7,1},{8,10},{9,11},{10,... | collective-permute-start | bytes 1179656 | tf_op jit(solution)/shard_map/ppermute | solution.py:305
  5.2 19.4 %collective-permute-start.20 = (bf16[48,4096]{1,0:T(8,128)(2,1)S(1)}, bf16[48,4096]{1,0:T(8,128)(2,1)}, u32[]{:S(2)}, u32[]{:S(2)}) collective-permute-start(bf16[48,4096]{1,0:T(8,128)(2,1)S(1)} %get-tuple-element.45), channel_id=1, source_target_pairs={{0,1},{1,0},{2,3},{3,2},{4,5},{5,4},{6,7},{7,6},{8,9},{9,8},{10,11... | collective-permute-start | bytes 1179656 | tf_op jit(solution)/shard_map/ppermute | solution.py:310
  16.2 24.1 %collective-permute-start.4 = (bf16[48,4096]{1,0:T(8,128)(2,1)}, bf16[48,4096]{1,0:T(8,128)(2,1)S(1)}, u32[]{:S(2)}, u32[]{:S(2)}) collective-permute-start(bf16[48,4096]{1,0:T(8,128)(2,1)} %collective-permute-done.3), channel_id=1, source_target_pairs={{0,2},{1,3},{2,4},{3,5},{4,6},{5,7},{6,0},{7,1},{8,10},{9,11},{10,... | collective-permute-start | bytes 1179656 | tf_op jit(solution)/shard_map/ppermute | solution.py:305
  16.2 25.4 %collective-permute-start.23 = (bf16[48,4096]{1,0:T(8,128)(2,1)}, bf16[48,4096]{1,0:T(8,128)(2,1)S(1)}, u32[]{:S(2)}, u32[]{:S(2)}) collective-permute-start(bf16[48,4096]{1,0:T(8,128)(2,1)} %collective-permute-done.3), channel_id=1, source_target_pairs={{0,1},{1,0},{2,3},{3,2},{4,5},{5,4},{6,7},{7,6},{8,9},{9,8},{10,11... | collective-permute-start | bytes 1179656 | tf_op jit(solution)/shard_map/ppermute | solution.py:310
  24.6 15.7 %collective-permute-start.1 = (bf16[48,4096]{1,0:T(8,128)(2,1)}, bf16[48,4096]{1,0:T(8,128)(2,1)S(1)}, u32[]{:S(2)}, u32[]{:S(2)}) collective-permute-start(bf16[48,4096]{1,0:T(8,128)(2,1)} %collective-permute-done), channel_id=1, source_target_pairs={{0,2},{1,3},{2,4},{3,5},{4,6},{5,7},{6,0},{7,1},{8,10},{9,11},{10,... | collective-permute-start | bytes 1179656 | tf_op jit(solution)/shard_map/ppermute | solution.py:305
  24.6 17.0 %collective-permute-start.22 = (bf16[48,4096]{1,0:T(8,128)(2,1)}, bf16[48,4096]{1,0:T(8,128)(2,1)S(1)}, u32[]{:S(2)}, u32[]{:S(2)}) collective-permute-start(bf16[48,4096]{1,0:T(8,128)(2,1)} %collective-permute-done), channel_id=1, source_target_pairs={{0,1},{1,0},{2,3},{3,2},{4,5},{5,4},{6,7},{7,6},{8,9},{9,8},{10,11... | collective-permute-start | bytes 1179656 | tf_op jit(solution)/shard_map/ppermute | solution.py:310
  40.3 20.3 %collective-permute-start.5 = (bf16[48,4096]{1,0:T(8,128)(2,1)S(1)}, bf16[48,4096]{1,0:T(8,128)(2,1)S(1)}, u32[]{:S(2)}, u32[]{:S(2)}) collective-permute-start(bf16[48,4096]{1,0:T(8,128)(2,1)S(1)} %collective-permute-done.4), channel_id=1, source_target_pairs={{0,2},{1,3},{2,4},{3,5},{4,6},{5,7},{6,0},{7,1},{8,10},{9,11},{10,... | collective-permute-start | bytes 1179656 | tf_op jit(solution)/shard_map/ppermute | solution.py:305
  44.6 16.7 %collective-permute-start.25 = (bf16[48,4096]{1,0:T(8,128)(2,1)S(1)}, bf16[48,4096]{1,0:T(8,128)(2,1)S(1)}, u32[]{:S(2)}, u32[]{:S(2)}) collective-permute-start(bf16[48,4096]{1,0:T(8,128)(2,1)S(1)} %collective-permute-done.4), channel_id=1, source_target_pairs={{0,1},{1,0},{2,3},{3,2},{4,5},{5,4},{6,7},{7,6},{8,9},{9,8},{10,11... | collective-permute-start | bytes 1179656 | tf_op jit(solution)/shard_map/ppermute | solution.py:310
  44.7 16.6 %collective-permute-start.24 = (bf16[48,4096]{1,0:T(8,128)(2,1)S(1)}, bf16[48,4096]{1,0:T(8,128)(2,1)S(1)}, u32[]{:S(2)}, u32[]{:S(2)}) collective-permute-start(bf16[48,4096]{1,0:T(8,128)(2,1)S(1)} %collective-permute-done.1), channel_id=1, source_target_pairs={{0,1},{1,0},{2,3},{3,2},{4,5},{5,4},{6,7},{7,6},{8,9},{9,8},{10,11... | collective-permute-start | bytes 1179656 | tf_op jit(solution)/shard_map/ppermute | solution.py:310
  60.7 17.4 %collective-permute-start.7 = (bf16[48,4096]{1,0:T(8,128)(2,1)S(1)}, bf16[48,4096]{1,0:T(8,128)(2,1)S(1)}, u32[]{:S(2)}, u32[]{:S(2)}) collective-permute-start(bf16[48,4096]{1,0:T(8,128)(2,1)S(1)} %get-tuple-element.44), channel_id=1, source_target_pairs={{0,1},{1,0},{2,3},{3,2},{4,5},{5,4},{6,7},{7,6},{8,9},{9,8},{10,11... | collective-permute-start | bytes 1179656 | tf_op jit(solution)/shard_map/ppermute | solution.py:310
  60.8 17.3 %collective-permute-start.6 = (bf16[48,4096]{1,0:T(8,128)(2,1)S(1)}, bf16[48,4096]{1,0:T(8,128)(2,1)S(1)}, u32[]{:S(2)}, u32[]{:S(2)}) collective-permute-start(bf16[48,4096]{1,0:T(8,128)(2,1)S(1)} %get-tuple-element.43), channel_id=1, source_target_pairs={{0,1},{1,0},{2,3},{3,2},{4,5},{5,4},{6,7},{7,6},{8,9},{9,8},{10,11... | collective-permute-start | bytes 1179656 | tf_op jit(solution)/shard_map/ppermute | solution.py:310
  61.3 21.2 %collective-permute-start.8 = (bf16[48,4096]{1,0:T(8,128)(2,1)S(1)}, bf16[48,4096]{1,0:T(8,128)(2,1)S(1)}, u32[]{:S(2)}, u32[]{:S(2)}) collective-permute-start(bf16[48,4096]{1,0:T(8,128)(2,1)S(1)} %get-tuple-element.43), channel_id=1, source_target_pairs={{0,2},{1,3},{2,4},{3,5},{4,6},{5,7},{6,0},{7,1},{8,10},{9,11},{10,... | collective-permute-start | bytes 1179656 | tf_op jit(solution)/shard_map/ppermute | solution.py:305
  78.0 16.4 %collective-permute-start.11 = (bf16[48,4096]{1,0:T(8,128)(2,1)S(1)}, bf16[48,4096]{1,0:T(8,128)(2,1)S(1)}, u32[]{:S(2)}, u32[]{:S(2)}) collective-permute-start(bf16[48,4096]{1,0:T(8,128)(2,1)S(1)} %collective-permute-done.9), channel_id=1, source_target_pairs={{0,1},{1,0},{2,3},{3,2},{4,5},{5,4},{6,7},{7,6},{8,9},{9,8},{10,11... | collective-permute-start | bytes 1179656 | tf_op jit(solution)/shard_map/ppermute | solution.py:310
  82.5 17.3 %collective-permute-start.12 = (bf16[48,4096]{1,0:T(8,128)(2,1)S(1)}, bf16[48,4096]{1,0:T(8,128)(2,1)S(1)}, u32[]{:S(2)}, u32[]{:S(2)}) collective-permute-start(bf16[48,4096]{1,0:T(8,128)(2,1)S(1)} %collective-permute-done.8), channel_id=1, source_target_pairs={{0,2},{1,3},{2,4},{3,5},{4,6},{5,7},{6,0},{7,1},{8,10},{9,11},{10,... | collective-permute-start | bytes 1179656 | tf_op jit(solution)/shard_map/ppermute | solution.py:305
  94.5 27.1 %collective-permute-start.15 = (bf16[48,4096]{1,0:T(8,128)(2,1)S(1)}, bf16[48,4096]{1,0:T(8,128)(2,1)S(1)}, u32[]{:S(2)}, u32[]{:S(2)}) collective-permute-start(bf16[48,4096]{1,0:T(8,128)(2,1)S(1)} %collective-permute-done.13), channel_id=1, source_target_pairs={{0,1},{1,0},{2,3},{3,2},{4,5},{5,4},{6,7},{7,6},{8,9},{9,8},{10,11... | collective-permute-start | bytes 1179656 | tf_op jit(solution)/shard_map/ppermute | solution.py:310
  99.8 21.8 %collective-permute-start.14 = (bf16[48,4096]{1,0:T(8,128)(2,1)S(1)}, bf16[48,4096]{1,0:T(8,128)(2,1)S(1)}, u32[]{:S(2)}, u32[]{:S(2)}) collective-permute-start(bf16[48,4096]{1,0:T(8,128)(2,1)S(1)} %collective-permute-done.12), channel_id=1, source_target_pairs={{0,1},{1,0},{2,3},{3,2},{4,5},{5,4},{6,7},{7,6},{8,9},{9,8},{10,11... | collective-permute-start | bytes 1179656 | tf_op jit(solution)/shard_map/ppermute | solution.py:310
  101.1 20.5 %collective-permute-start.18 = (bf16[48,4096]{1,0:T(8,128)(2,1)S(1)}, bf16[48,4096]{1,0:T(8,128)(2,1)S(1)}, u32[]{:S(2)}, u32[]{:S(2)}) collective-permute-start(bf16[48,4096]{1,0:T(8,128)(2,1)S(1)} %collective-permute-done.13), channel_id=1, source_target_pairs={{0,2},{1,3},{2,4},{3,5},{4,6},{5,7},{6,0},{7,1},{8,10},{9,11},{10,... | collective-permute-start | bytes 1179656 | tf_op jit(solution)/shard_map/ppermute | solution.py:305
  173.3 19.2 %collective-permute-start.45 = (bf16[48,4096]{1,0:T(8,128)(2,1)S(1)}, bf16[48,4096]{1,0:T(8,128)(2,1)S(1)}, u32[]{:S(2)}, u32[]{:S(2)}) collective-permute-start(bf16[48,4096]{1,0:T(8,128)(2,1)S(1)} %add_convert_fusion.7), channel_id=1, source_target_pairs={{0,2},{1,3},{2,4},{3,5},{4,6},{5,7},{6,0},{7,1},{8,10},{9,11},{10,... | collective-permute-start | bytes 1179656 | tf_op jit(solution)/shard_map/ppermute | solution.py:305
  184.2 16.7 %collective-permute-start.43 = (bf16[48,4096]{1,0:T(8,128)(2,1)S(1)}, bf16[48,4096]{1,0:T(8,128)(2,1)S(1)}, u32[]{:S(2)}, u32[]{:S(2)}) collective-permute-start(bf16[48,4096]{1,0:T(8,128)(2,1)S(1)} %add_convert_fusion.5), channel_id=1, source_target_pairs={{0,2},{1,3},{2,4},{3,5},{4,6},{5,7},{6,0},{7,1},{8,10},{9,11},{10,... | collective-permute-start | bytes 1179656 | tf_op jit(solution)/shard_map/ppermute | solution.py:305
  192.6 16.7 %collective-permute-start.46 = (bf16[48,4096]{1,0:T(8,128)(2,1)S(1)}, bf16[48,4096]{1,0:T(8,128)(2,1)S(1)}, u32[]{:S(2)}, u32[]{:S(2)}) collective-permute-start(bf16[48,4096]{1,0:T(8,128)(2,1)S(1)} %add_convert_fusion.2), channel_id=1, source_target_pairs={{0,2},{1,3},{2,4},{3,5},{4,6},{5,7},{6,0},{7,1},{8,10},{9,11},{10,... | collective-permute-start | bytes 1179656 | tf_op jit(solution)/shard_map/ppermute | solution.py:305
  201.1 16.7 %collective-permute-start.44 = (bf16[48,4096]{1,0:T(8,128)(2,1)S(1)}, bf16[48,4096]{1,0:T(8,128)(2,1)S(1)}, u32[]{:S(2)}, u32[]{:S(2)}) collective-permute-start(bf16[48,4096]{1,0:T(8,128)(2,1)S(1)} %add_convert_fusion.4), channel_id=1, source_target_pairs={{0,2},{1,3},{2,4},{3,5},{4,6},{5,7},{6,0},{7,1},{8,10},{9,11},{10,... | collective-permute-start | bytes 1179656 | tf_op jit(solution)/shard_map/ppermute | solution.py:305
  209.5 15.8 %collective-permute-start.47 = (bf16[48,4096]{1,0:T(8,128)(2,1)S(1)}, bf16[48,4096]{1,0:T(8,128)(2,1)S(1)}, u32[]{:S(2)}, u32[]{:S(2)}) collective-permute-start(bf16[48,4096]{1,0:T(8,128)(2,1)S(1)} %add_convert_fusion.1), channel_id=1, source_target_pairs={{0,2},{1,3},{2,4},{3,5},{4,6},{5,7},{6,0},{7,1},{8,10},{9,11},{10,... | collective-permute-start | bytes 1179656 | tf_op jit(solution)/shard_map/ppermute | solution.py:305
  (48 other events, 478.9 us)

commit v2 on v1

--- a/solution.py
+++ b/solution.py
@@ -368,7 +368,7 @@
 
 def multiply_rows(rows, weight):
     depth, inner = weight.shape
-    block = math.gcd(depth, 512)
+    block = math.gcd(depth, 1024)
     count = rows.shape[0] // 2
     out = pl.BlockSpec((count, block), lambda i: (0, i))
     return pl.pallas_call(
@@ -445,7 +445,7 @@
         jnp.zeros((length, weight_cat.shape[1]), BF16),
     )
     local, grads_in = ring_gather(
-        [after(out_grad[at : at + size], rows_in[-1][i]) for i, (at, size) in enumerate(cuts)],
+        [after(out_grad[at : at + size], (rows_in[-2][1], rows_in[-1][0])[i] if len(rows_in) > 1 else rows_in[-1][i]) for i, (at, size) in enumerate(cuts)],
         multiply_into(out_weight, (1, 1), held, F32),
         jnp.zeros((length, width), F32),
     )

time: 227 us -> 220 us (0.969)
  waiting for transfers between devices: 128 us -> 124 us
    ppermute x27, waiting for transfers between devices: 126 us -> 122 us  [turned(): lax.ppermute(value, axis, [(i, (i + by) % length) for i in range(length)])]
  transfers between devices with their start and end apart: 48 -> 48, of which waited for: 25 -> 24; matrix products, arithmetic and copies ran while one was open for 11% -> 12% of each run, Pallas kernels for 9% -> 9%
where the time goes in v2:
time: 220 us
  waiting for transfers between devices  124 us (56%)
  starting transfers between devices  28.9 us (13%)
  Pallas kernels  28.6 us (13%)
  matrix products  16.9 us (8%)
  local copies, waits for them, and re-layouts  13.6 us (6%)
  other arithmetic  7.05 us (3%)
    ppermute x27, waiting for transfers between devices, turned(): lax.ppermute(value, axis, [(i, (i + by) % length) for i in range(length)])  122 us
    ppermute x27, starting transfers between devices, turned(): lax.ppermute(value, axis, [(i, (i + by) % length) for i in range(length)])  18.8 us
    dot_general x10, matrix products, dot(): lax.dot_general(a, b, (((over[0],), (over[1],)), ((), ())), precision=pre...  16.9 us
    pallas_call x2, Pallas kernels, multiply_rows(): pl.pallas_call(product_rows, grid=(depth // block,), in_specs=[pl.BlockSp...  8.46 us
    unnamed x64, local copies, waits for them, and re-layouts  8.19 us
    ppermute x2, starting transfers between devices, shifted(): return lax.ppermute(value, axis, pairs)  7.36 us
    pallas_call x1, Pallas kernels, body(): pl.pallas_call(partial(backward_carried, heads, block), out_shape=[shape(...  5.11 us
    pallas_call x1, Pallas kernels, body(): pl.pallas_call(partial(forward_local, heads, block), out_shape=[shape(len...  4.79 us
  transfers between devices with their start and end apart: 48, of which 24 were waited for; matrix products, arithmetic and copies ran while one was open for 12% of the time, Pallas kernels for 9%

profile of v2, /device:TPU:4, one launch (start us, length us, event | category | flops | bytes accessed | tf_op | source)
XLA Modules:
  0.0 219.6 jit_solution(12471610245341730334)
XLA Ops:
  12.3 3.9 %collective-permute-done = bf16[48,4096]{1,0:T(8,128)(2,1)} collective-permute-done((bf16[48,4096]{1,0:T(8,128)(2,1)}, bf16[48,4096]{1,0:T(8,128)(2,1)}, u32[]{:S(2)}, u32[]{:S(2)}) %collective-permute-start) | collective-permute-done | bytes 393248 | tf_op jit(solution)/shard_map/ppermute | solution.py:305
  16.2 8.4 %collective-permute-done.2 = bf16[48,4096]{1,0:T(8,128)(2,1)} collective-permute-done((bf16[48,4096]{1,0:T(8,128)(2,1)S(1)}, bf16[48,4096]{1,0:T(8,128)(2,1)}, u32[]{:S(2)}, u32[]{:S(2)}) %collective-permute-start.2) | collective-permute-done | bytes 393248 | tf_op jit(solution)/shard_map/ppermute | solution.py:305
  24.6 5.5 %fusion.48 = bf16[192,896]{1,0:T(8,128)(2,1)S(1)} fusion(bf16[4096,896]{1,0:T(8,128)(2,1)} %fusion.1.weight, bf16[48,4096]{1,0:T(8,128)(2,1)} %collective-permute-done.20, bf16[48,4096]{1,0:T(8,128)(2,1)} %collective-permute-done.19, bf16[96,4096]{1,0:T(8,128)(2,1)} %param.11), kind=kOutput, calls=%fused_computation.51 | convolution fusion | flops 1414176768 | bytes 9256960 | tf_op jit(solution)/shard_map/dot_general | solution.py:28
  30.4 9.9 %collective-permute-done.3 = bf16[48,4096]{1,0:T(8,128)(2,1)S(1)} collective-permute-done((bf16[48,4096]{1,0:T(8,128)(2,1)}, bf16[48,4096]{1,0:T(8,128)(2,1)S(1)}, u32[]{:S(2)}, u32[]{:S(2)}) %collective-permute-start.3) | collective-permute-done | bytes 393248 | tf_op jit(solution)/shard_map/ppermute | solution.py:305
  45.2 8.9 %collective-permute-done.4 = bf16[48,4096]{1,0:T(8,128)(2,1)S(1)} collective-permute-done((bf16[48,4096]{1,0:T(8,128)(2,1)S(1)}, bf16[48,4096]{1,0:T(8,128)(2,1)S(1)}, u32[]{:S(2)}, u32[]{:S(2)}) %collective-permute-start.4) | collective-permute-done | bytes 393248 | tf_op jit(solution)/shard_map/ppermute | solution.py:305
  56.9 4.9 %collective-permute-done.26 = bf16[48,4096]{1,0:T(8,128)(2,1)S(1)} collective-permute-done((bf16[48,4096]{1,0:T(8,128)(2,1)S(1)}, bf16[48,4096]{1,0:T(8,128)(2,1)S(1)}, u32[]{:S(2)}, u32[]{:S(2)}) %collective-permute-start.26) | collective-permute-done | bytes 393248 | tf_op jit(solution)/shard_map/ppermute | solution.py:305
  64.9 5.4 %collective-permute-done.8 = bf16[48,4096]{1,0:T(8,128)(2,1)S(1)} collective-permute-done((bf16[48,4096]{1,0:T(8,128)(2,1)S(1)}, bf16[48,4096]{1,0:T(8,128)(2,1)S(1)}, u32[]{:S(2)}, u32[]{:S(2)}) %collective-permute-start.8) | collective-permute-done | bytes 393248 | tf_op jit(solution)/shard_map/ppermute | solution.py:305
  77.5 4.8 %forward_local.1 = (bf16[768,1280]{1,0:T(8,128)(2,1)S(1)}, f32[768,896]{1,0:T(8,128)S(1)}, f32[768,256]{1,0:T(8,128)S(1)}, f32[1536,128]{1,0:T(8,128)S(1)}, f32[256,128]{1,0:T(8,128)S(1)}) custom-call(bf16[768,896]{1,0:T(8,128)(2,1)S(1)} %slice_dynamic-update-slice_fusion.12.proj, bf16[8,512]{1,0:T(8,128)(2,1)S(1)} %broadcast_add_fusion.tail, ...), custom_call_target="tpu_custom_call" | custom-call | flops 1000 | bytes 1000 | tf_op jit(solution)/shard_map/forward_local/pallas_call | solution.py:455
  82.4 5.2 %collective-permute-done.12 = bf16[48,4096]{1,0:T(8,128)(2,1)S(1)} collective-permute-done((bf16[48,4096]{1,0:T(8,128)(2,1)S(1)}, bf16[48,4096]{1,0:T(8,128)(2,1)S(1)}, u32[]{:S(2)}, u32[]{:S(2)}) %collective-permute-start.12) | collective-permute-done | bytes 393248 | tf_op jit(solution)/shard_map/ppermute | solution.py:305
  91.1 4.4 %collective-permute-done.11 = bf16[48,4096]{1,0:T(8,128)(2,1)S(1)} collective-permute-done((bf16[48,4096]{1,0:T(8,128)(2,1)S(1)}, bf16[48,4096]{1,0:T(8,128)(2,1)S(1)}, u32[]{:S(2)}, u32[]{:S(2)}) %collective-permute-start.11) | collective-permute-done | bytes 393248 | tf_op jit(solution)/shard_map/ppermute | solution.py:305
  97.1 3.5 %forward_carried.1 = (f32[768,768]{1,0:T(8,128)S(1)}, bf16[768,512]{1,0:T(8,128)(2,1)S(1)}, f32[8,768]{1,0:T(8,128)S(1)}) custom-call(bf16[768,896]{1,0:T(8,128)(2,1)S(1)} %slice_dynamic-update-slice_fusion.12.proj, bf16[768,1280]{1,0:T(8,128)(2,1)S(1)} %get-tuple-element.23.saved, f32[768,896]{1,0:T(8,128)S(1)} %get-tuple-element.24.factors, ...), custom_call_target="tpu_custom_call" | custom-call | flops 1000 | bytes 1000 | tf_op jit(solution)/shard_map/forward_carried/pallas_call | solution.py:492
  100.6 8.7 %collective-permute-done.15 = bf16[48,4096]{1,0:T(8,128)(2,1)S(1)} collective-permute-done((bf16[48,4096]{1,0:T(8,128)(2,1)S(1)}, bf16[48,4096]{1,0:T(8,128)(2,1)S(1)}, u32[]{:S(2)}, u32[]{:S(2)}) %collective-permute-start.15) | collective-permute-done | bytes 393248 | tf_op jit(solution)/shard_map/ppermute | solution.py:305
  109.3 8.0 %collective-permute-done.17 = bf16[48,4096]{1,0:T(8,128)(2,1)S(1)} collective-permute-done((bf16[48,4096]{1,0:T(8,128)(2,1)S(1)}, bf16[48,4096]{1,0:T(8,128)(2,1)S(1)}, u32[]{:S(2)}, u32[]{:S(2)}) %collective-permute-start.17) | collective-permute-done | bytes 393248 | tf_op jit(solution)/shard_map/ppermute | solution.py:305
  122.1 3.7 %collective-permute-start.35 = (f32[8,768]{1,0:T(8,128)S(1)}, f32[8,768]{1,0:T(8,128)S(1)}, u32[]{:S(2)}, u32[]{:S(2)}) collective-permute-start(f32[8,768]{1,0:T(8,128)S(1)} %add.441.refs_0_), channel_id=1, source_target_pairs={{0,6},{1,7},{2,0},{3,1},{4,2},{5,3},{6,4},{7,5},{8,14},{9,15},{10,... | collective-permute-start | bytes 73736 | tf_op jit(solution)/shard_map/ppermute | solution.py:305
  141.2 5.1 %backward_carried.1 = (bf16[768,896]{1,0:T(8,128)(2,1)S(1)}, f32[8,512]{1,0:T(8,128)S(1)}, f32[8,512]{1,0:T(8,128)}) custom-call(bf16[768,768]{1,0:T(8,128)(2,1)S(1)} %get-tuple-element.30.cots, bf16[768,1280]{1,0:T(8,128)(2,1)S(1)} %copy-done.5, f32[768,896]{1,0:T(8,128)S(1)} %copy-done.7, f32[1,128]{1,0:T(1,128)S(1)} %get-tuple-element.51.rate, ...), custom_call_target="tpu_custom_call" | custom-call | flops 1000 | bytes 1000 | tf_op jit(solution)/shard_map/backward_carried/pallas_call | solution.py:530
  146.9 4.0 %collective-permute-start.40 = (f32[8,512]{1,0:T(8,128)}, f32[8,512]{1,0:T(8,128)S(1)}, u32[]{:S(2)}, u32[]{:S(2)}) collective-permute-start(f32[8,512]{1,0:T(8,128)} %get-tuple-element.38), channel_id=1, source_target_pairs={{8,0},{16,8},{24,16},{9,1},{17,9},{25,17},{10,2},{18,10},{26,18},{... | collective-permute-start | bytes 49160 | tf_op jit(solution)/shard_map/ppermute | solution.py:316
  154.0 4.2 %product_rows.2 = (bf16[192,4096]{1,0:T(8,128)(2,1)S(1)}, bf16[192,4096]{1,0:T(8,128)(2,1)S(1)}) custom-call(bf16[384,896]{1,0:T(8,128)(2,1)S(1)} %dynamic-slice_dynamic-update-slice_fusion.8.rows, bf16[4096,896]{1,0:T(8,128)(2,1)S(1)} %copy-done.2), custom_call_target="tpu_custom_call" | custom-call | flops 1000 | bytes 1000 | tf_op jit(solution)/shard_map/product_rows/pallas_call | solution.py:374
  158.6 4.2 %product_rows.3 = (bf16[192,4096]{1,0:T(8,128)(2,1)S(1)}, bf16[192,4096]{1,0:T(8,128)(2,1)S(1)}) custom-call(bf16[384,896]{1,0:T(8,128)(2,1)S(1)} %dynamic-slice_dynamic-update-slice_fusion.rows, bf16[4096,896]{1,0:T(8,128)(2,1)S(1)} %copy-done.2), custom_call_target="tpu_custom_call" | custom-call | flops 1000 | bytes 1000 | tf_op jit(solution)/shard_map/product_rows/pallas_call | solution.py:374
  168.6 8.7 %collective-permute-done.42 = bf16[48,4096]{1,0:T(8,128)(2,1)S(1)} collective-permute-done((bf16[48,4096]{1,0:T(8,128)(2,1)S(1)}, bf16[48,4096]{1,0:T(8,128)(2,1)S(1)}, u32[]{:S(2)}, u32[]{:S(2)}) %collective-permute-start.42) | collective-permute-done | bytes 393248 | tf_op jit(solution)/shard_map/ppermute | solution.py:305
  177.8 8.0 %collective-permute-done.45 = bf16[48,4096]{1,0:T(8,128)(2,1)S(1)} collective-permute-done((bf16[48,4096]{1,0:T(8,128)(2,1)S(1)}, bf16[48,4096]{1,0:T(8,128)(2,1)S(1)}, u32[]{:S(2)}, u32[]{:S(2)}) %collective-permute-start.45) | collective-permute-done | bytes 393248 | tf_op jit(solution)/shard_map/ppermute | solution.py:305
  186.2 8.0 %collective-permute-done.43 = bf16[48,4096]{1,0:T(8,128)(2,1)S(1)} collective-permute-done((bf16[48,4096]{1,0:T(8,128)(2,1)S(1)}, bf16[48,4096]{1,0:T(8,128)(2,1)S(1)}, u32[]{:S(2)}, u32[]{:S(2)}) %collective-permute-start.43) | collective-permute-done | bytes 393248 | tf_op jit(solution)/shard_map/ppermute | solution.py:305
  194.6 8.0 %collective-permute-done.46 = bf16[48,4096]{1,0:T(8,128)(2,1)S(1)} collective-permute-done((bf16[48,4096]{1,0:T(8,128)(2,1)S(1)}, bf16[48,4096]{1,0:T(8,128)(2,1)S(1)}, u32[]{:S(2)}, u32[]{:S(2)}) %collective-permute-start.46) | collective-permute-done | bytes 393248 | tf_op jit(solution)/shard_map/ppermute | solution.py:305
  203.0 8.0 %collective-permute-done.44 = bf16[48,4096]{1,0:T(8,128)(2,1)S(1)} collective-permute-done((bf16[48,4096]{1,0:T(8,128)(2,1)S(1)}, bf16[48,4096]{1,0:T(8,128)(2,1)S(1)}, u32[]{:S(2)}, u32[]{:S(2)}) %collective-permute-start.44) | collective-permute-done | bytes 393248 | tf_op jit(solution)/shard_map/ppermute | solution.py:305
  211.2 7.4 %collective-permute-done.47 = bf16[48,4096]{1,0:T(8,128)(2,1)S(1)} collective-permute-done((bf16[48,4096]{1,0:T(8,128)(2,1)S(1)}, bf16[48,4096]{1,0:T(8,128)(2,1)S(1)}, u32[]{:S(2)}, u32[]{:S(2)}) %collective-permute-start.47) | collective-permute-done | bytes 393248 | tf_op jit(solution)/shard_map/ppermute | solution.py:305
  (217 shorter events, 68.0 us)
Async XLA Ops:
  2.1 14.1 %collective-permute-start = (bf16[48,4096]{1,0:T(8,128)(2,1)}, bf16[48,4096]{1,0:T(8,128)(2,1)}, u32[]{:S(2)}, u32[]{:S(2)}) collective-permute-start(bf16[48,4096]{1,0:T(8,128)(2,1)} %get-tuple-element.45), channel_id=1, source_target_pairs={{0,2},{1,3},{2,4},{3,5},{4,6},{5,7},{6,0},{7,1},{8,10},{9,11},{10,... | collective-permute-start | bytes 1179656 | tf_op jit(solution)/shard_map/ppermute | solution.py:305
  3.7 21.0 %collective-permute-start.20 = (bf16[48,4096]{1,0:T(8,128)(2,1)}, bf16[48,4096]{1,0:T(8,128)(2,1)}, u32[]{:S(2)}, u32[]{:S(2)}) collective-permute-start(bf16[48,4096]{1,0:T(8,128)(2,1)} %get-tuple-element.45), channel_id=1, source_target_pairs={{0,1},{1,0},{2,3},{3,2},{4,5},{5,4},{6,7},{7,6},{8,9},{9,8},{10,11... | collective-permute-start | bytes 1179656 | tf_op jit(solution)/shard_map/ppermute | solution.py:310
  3.7 21.0 %collective-permute-start.2 = (bf16[48,4096]{1,0:T(8,128)(2,1)S(1)}, bf16[48,4096]{1,0:T(8,128)(2,1)}, u32[]{:S(2)}, u32[]{:S(2)}) collective-permute-start(bf16[48,4096]{1,0:T(8,128)(2,1)S(1)} %get-tuple-element.46), channel_id=1, source_target_pairs={{0,2},{1,3},{2,4},{3,5},{4,6},{5,7},{6,0},{7,1},{8,10},{9,11},{10,... | collective-permute-start | bytes 1179656 | tf_op jit(solution)/shard_map/ppermute | solution.py:305
  5.2 19.4 %collective-permute-start.19 = (bf16[48,4096]{1,0:T(8,128)(2,1)S(1)}, bf16[48,4096]{1,0:T(8,128)(2,1)}, u32[]{:S(2)}, u32[]{:S(2)}) collective-permute-start(bf16[48,4096]{1,0:T(8,128)(2,1)S(1)} %get-tuple-element.46), channel_id=1, source_target_pairs={{0,1},{1,0},{2,3},{3,2},{4,5},{5,4},{6,7},{7,6},{8,9},{9,8},{10,11... | collective-permute-start | bytes 1179656 | tf_op jit(solution)/shard_map/ppermute | solution.py:310
  16.2 27.2 %collective-permute-start.1 = (bf16[48,4096]{1,0:T(8,128)(2,1)}, bf16[48,4096]{1,0:T(8,128)(2,1)S(1)}, u32[]{:S(2)}, u32[]{:S(2)}) collective-permute-start(bf16[48,4096]{1,0:T(8,128)(2,1)} %collective-permute-done), channel_id=1, source_target_pairs={{0,2},{1,3},{2,4},{3,5},{4,6},{5,7},{6,0},{7,1},{8,10},{9,11},{10,... | collective-permute-start | bytes 1179656 | tf_op jit(solution)/shard_map/ppermute | solution.py:305
  16.2 24.1 %collective-permute-start.22 = (bf16[48,4096]{1,0:T(8,128)(2,1)}, bf16[48,4096]{1,0:T(8,128)(2,1)S(1)}, u32[]{:S(2)}, u32[]{:S(2)}) collective-permute-start(bf16[48,4096]{1,0:T(8,128)(2,1)} %collective-permute-done), channel_id=1, source_target_pairs={{0,1},{1,0},{2,3},{3,2},{4,5},{5,4},{6,7},{7,6},{8,9},{9,8},{10,11... | collective-permute-start | bytes 1179656 | tf_op jit(solution)/shard_map/ppermute | solution.py:310
  24.6 15.7 %collective-permute-start.3 = (bf16[48,4096]{1,0:T(8,128)(2,1)}, bf16[48,4096]{1,0:T(8,128)(2,1)S(1)}, u32[]{:S(2)}, u32[]{:S(2)}) collective-permute-start(bf16[48,4096]{1,0:T(8,128)(2,1)} %collective-permute-done.2), channel_id=1, source_target_pairs={{0,2},{1,3},{2,4},{3,5},{4,6},{5,7},{6,0},{7,1},{8,10},{9,11},{10,... | collective-permute-start | bytes 1179656 | tf_op jit(solution)/shard_map/ppermute | solution.py:305
  24.6 15.7 %collective-permute-start.21 = (bf16[48,4096]{1,0:T(8,128)(2,1)}, bf16[48,4096]{1,0:T(8,128)(2,1)S(1)}, u32[]{:S(2)}, u32[]{:S(2)}) collective-permute-start(bf16[48,4096]{1,0:T(8,128)(2,1)} %collective-permute-done.2), channel_id=1, source_target_pairs={{0,1},{1,0},{2,3},{3,2},{4,5},{5,4},{6,7},{7,6},{8,9},{9,8},{10,11... | collective-permute-start | bytes 1179656 | tf_op jit(solution)/shard_map/ppermute | solution.py:310
  40.3 13.8 %collective-permute-start.4 = (bf16[48,4096]{1,0:T(8,128)(2,1)S(1)}, bf16[48,4096]{1,0:T(8,128)(2,1)S(1)}, u32[]{:S(2)}, u32[]{:S(2)}) collective-permute-start(bf16[48,4096]{1,0:T(8,128)(2,1)S(1)} %collective-permute-done.3), channel_id=1, source_target_pairs={{0,2},{1,3},{2,4},{3,5},{4,6},{5,7},{6,0},{7,1},{8,10},{9,11},{10,... | collective-permute-start | bytes 1179656 | tf_op jit(solution)/shard_map/ppermute | solution.py:305
  43.9 18.0 %collective-permute-start.26 = (bf16[48,4096]{1,0:T(8,128)(2,1)S(1)}, bf16[48,4096]{1,0:T(8,128)(2,1)S(1)}, u32[]{:S(2)}, u32[]{:S(2)}) collective-permute-start(bf16[48,4096]{1,0:T(8,128)(2,1)S(1)} %collective-permute-done.1), channel_id=1, source_target_pairs={{0,2},{1,3},{2,4},{3,5},{4,6},{5,7},{6,0},{7,1},{8,10},{9,11},{10,... | collective-permute-start | bytes 1179656 | tf_op jit(solution)/shard_map/ppermute | solution.py:305
  54.3 19.5 %collective-permute-start.6 = (bf16[48,4096]{1,0:T(8,128)(2,1)S(1)}, bf16[48,4096]{1,0:T(8,128)(2,1)S(1)}, u32[]{:S(2)}, u32[]{:S(2)}) collective-permute-start(bf16[48,4096]{1,0:T(8,128)(2,1)S(1)} %get-tuple-element.44), channel_id=1, source_target_pairs={{0,1},{1,0},{2,3},{3,2},{4,5},{5,4},{6,7},{7,6},{8,9},{9,8},{10,11... | collective-permute-start | bytes 1179656 | tf_op jit(solution)/shard_map/ppermute | solution.py:310
  54.3 15.9 %collective-permute-start.8 = (bf16[48,4096]{1,0:T(8,128)(2,1)S(1)}, bf16[48,4096]{1,0:T(8,128)(2,1)S(1)}, u32[]{:S(2)}, u32[]{:S(2)}) collective-permute-start(bf16[48,4096]{1,0:T(8,128)(2,1)S(1)} %get-tuple-element.44), channel_id=1, source_target_pairs={{0,2},{1,3},{2,4},{3,5},{4,6},{5,7},{6,0},{7,1},{8,10},{9,11},{10,... | collective-permute-start | bytes 1179656 | tf_op jit(solution)/shard_map/ppermute | solution.py:305
  54.4 19.4 %collective-permute-start.5 = (bf16[48,4096]{1,0:T(8,128)(2,1)S(1)}, bf16[48,4096]{1,0:T(8,128)(2,1)S(1)}, u32[]{:S(2)}, u32[]{:S(2)}) collective-permute-start(bf16[48,4096]{1,0:T(8,128)(2,1)S(1)} %get-tuple-element.43), channel_id=1, source_target_pairs={{0,1},{1,0},{2,3},{3,2},{4,5},{5,4},{6,7},{7,6},{8,9},{9,8},{10,11... | collective-permute-start | bytes 1179656 | tf_op jit(solution)/shard_map/ppermute | solution.py:310
  61.8 15.6 %collective-permute-start.7 = (bf16[48,4096]{1,0:T(8,128)(2,1)S(1)}, bf16[48,4096]{1,0:T(8,128)(2,1)S(1)}, u32[]{:S(2)}, u32[]{:S(2)}) collective-permute-start(bf16[48,4096]{1,0:T(8,128)(2,1)S(1)} %get-tuple-element.43), channel_id=1, source_target_pairs={{0,2},{1,3},{2,4},{3,5},{4,6},{5,7},{6,0},{7,1},{8,10},{9,11},{10,... | collective-permute-start | bytes 1179656 | tf_op jit(solution)/shard_map/ppermute | solution.py:305
  73.7 16.0 %collective-permute-start.10 = (bf16[48,4096]{1,0:T(8,128)(2,1)S(1)}, bf16[48,4096]{1,0:T(8,128)(2,1)S(1)}, u32[]{:S(2)}, u32[]{:S(2)}) collective-permute-start(bf16[48,4096]{1,0:T(8,128)(2,1)S(1)} %collective-permute-done.8), channel_id=1, source_target_pairs={{0,1},{1,0},{2,3},{3,2},{4,5},{5,4},{6,7},{7,6},{8,9},{9,8},{10,11... | collective-permute-start | bytes 1179656 | tf_op jit(solution)/shard_map/ppermute | solution.py:310
  77.4 18.1 %collective-permute-start.11 = (bf16[48,4096]{1,0:T(8,128)(2,1)S(1)}, bf16[48,4096]{1,0:T(8,128)(2,1)S(1)}, u32[]{:S(2)}, u32[]{:S(2)}) collective-permute-start(bf16[48,4096]{1,0:T(8,128)(2,1)S(1)} %collective-permute-done.7), channel_id=1, source_target_pairs={{0,2},{1,3},{2,4},{3,5},{4,6},{5,7},{6,0},{7,1},{8,10},{9,11},{10,... | collective-permute-start | bytes 1179656 | tf_op jit(solution)/shard_map/ppermute | solution.py:305
  90.2 27.1 %collective-permute-start.14 = (bf16[48,4096]{1,0:T(8,128)(2,1)S(1)}, bf16[48,4096]{1,0:T(8,128)(2,1)S(1)}, u32[]{:S(2)}, u32[]{:S(2)}) collective-permute-start(bf16[48,4096]{1,0:T(8,128)(2,1)S(1)} %collective-permute-done.12), channel_id=1, source_target_pairs={{0,1},{1,0},{2,3},{3,2},{4,5},{5,4},{6,7},{7,6},{8,9},{9,8},{10,11... | collective-permute-start | bytes 1179656 | tf_op jit(solution)/shard_map/ppermute | solution.py:310
  95.5 21.8 %collective-permute-start.13 = (bf16[48,4096]{1,0:T(8,128)(2,1)S(1)}, bf16[48,4096]{1,0:T(8,128)(2,1)S(1)}, u32[]{:S(2)}, u32[]{:S(2)}) collective-permute-start(bf16[48,4096]{1,0:T(8,128)(2,1)S(1)} %collective-permute-done.11), channel_id=1, source_target_pairs={{0,1},{1,0},{2,3},{3,2},{4,5},{5,4},{6,7},{7,6},{8,9},{9,8},{10,11... | collective-permute-start | bytes 1179656 | tf_op jit(solution)/shard_map/ppermute | solution.py:310
  96.4 20.9 %collective-permute-start.17 = (bf16[48,4096]{1,0:T(8,128)(2,1)S(1)}, bf16[48,4096]{1,0:T(8,128)(2,1)S(1)}, u32[]{:S(2)}, u32[]{:S(2)}) collective-permute-start(bf16[48,4096]{1,0:T(8,128)(2,1)S(1)} %collective-permute-done.12), channel_id=1, source_target_pairs={{0,2},{1,3},{2,4},{3,5},{4,6},{5,7},{6,0},{7,1},{8,10},{9,11},{10,... | collective-permute-start | bytes 1179656 | tf_op jit(solution)/shard_map/ppermute | solution.py:305
  166.5 19.2 %collective-permute-start.45 = (bf16[48,4096]{1,0:T(8,128)(2,1)S(1)}, bf16[48,4096]{1,0:T(8,128)(2,1)S(1)}, u32[]{:S(2)}, u32[]{:S(2)}) collective-permute-start(bf16[48,4096]{1,0:T(8,128)(2,1)S(1)} %add_convert_fusion.7), channel_id=1, source_target_pairs={{0,2},{1,3},{2,4},{3,5},{4,6},{5,7},{6,0},{7,1},{8,10},{9,11},{10,... | collective-permute-start | bytes 1179656 | tf_op jit(solution)/shard_map/ppermute | solution.py:305
  177.5 16.7 %collective-permute-start.43 = (bf16[48,4096]{1,0:T(8,128)(2,1)S(1)}, bf16[48,4096]{1,0:T(8,128)(2,1)S(1)}, u32[]{:S(2)}, u32[]{:S(2)}) collective-permute-start(bf16[48,4096]{1,0:T(8,128)(2,1)S(1)} %add_convert_fusion.5), channel_id=1, source_target_pairs={{0,2},{1,3},{2,4},{3,5},{4,6},{5,7},{6,0},{7,1},{8,10},{9,11},{10,... | collective-permute-start | bytes 1179656 | tf_op jit(solution)/shard_map/ppermute | solution.py:305
  185.9 16.7 %collective-permute-start.46 = (bf16[48,4096]{1,0:T(8,128)(2,1)S(1)}, bf16[48,4096]{1,0:T(8,128)(2,1)S(1)}, u32[]{:S(2)}, u32[]{:S(2)}) collective-permute-start(bf16[48,4096]{1,0:T(8,128)(2,1)S(1)} %add_convert_fusion.2), channel_id=1, source_target_pairs={{0,2},{1,3},{2,4},{3,5},{4,6},{5,7},{6,0},{7,1},{8,10},{9,11},{10,... | collective-permute-start | bytes 1179656 | tf_op jit(solution)/shard_map/ppermute | solution.py:305
  194.3 16.7 %collective-permute-start.44 = (bf16[48,4096]{1,0:T(8,128)(2,1)S(1)}, bf16[48,4096]{1,0:T(8,128)(2,1)S(1)}, u32[]{:S(2)}, u32[]{:S(2)}) collective-permute-start(bf16[48,4096]{1,0:T(8,128)(2,1)S(1)} %add_convert_fusion.4), channel_id=1, source_target_pairs={{0,2},{1,3},{2,4},{3,5},{4,6},{5,7},{6,0},{7,1},{8,10},{9,11},{10,... | collective-permute-start | bytes 1179656 | tf_op jit(solution)/shard_map/ppermute | solution.py:305
  202.8 15.8 %collective-permute-start.47 = (bf16[48,4096]{1,0:T(8,128)(2,1)S(1)}, bf16[48,4096]{1,0:T(8,128)(2,1)S(1)}, u32[]{:S(2)}, u32[]{:S(2)}) collective-permute-start(bf16[48,4096]{1,0:T(8,128)(2,1)S(1)} %add_convert_fusion.1), channel_id=1, source_target_pairs={{0,2},{1,3},{2,4},{3,5},{4,6},{5,7},{6,0},{7,1},{8,10},{9,11},{10,... | collective-permute-start | bytes 1179656 | tf_op jit(solution)/shard_map/ppermute | solution.py:305
  (48 other events, 462.8 us)

commit v3 on v2

--- a/solution.py
+++ b/solution.py
@@ -471,6 +471,7 @@
     total_log = jnp.sum(ends, axis=0)
     message = jnp.concatenate([own, jnp.broadcast_to(jnp.pad(total_log, (0, LANES - heads)), (8, LANES))], axis=0)
     second = grads_in[min(1, len(grads_in) - 1)]
+    third = grads_in[min(2, len(grads_in) - 1)]
     message = after(message, second[1])
     received = [turned(message, "ctx", by) for by in range(1, shards)]
     logs = [part[heads * HEAD_DIM, :heads] for part in received]
@@ -498,7 +499,7 @@
         ],
         name="forward_carried",
         **PARAMS,
-    )(proj, saved, factors, diag, states, after(spread(entering_weights), second[0]), *received)
+    )(proj, saved, factors, diag, states, after(after(spread(entering_weights), second[0]), third[0]), *received)
 
     sums = pl.pallas_call(token_sums, out_shape=shape(8, length), name="token_sums", **PARAMS)(
         local, gain, gates, squares

time: 220 us -> 219 us (level)
  transfers between devices with their start and end apart: 48 -> 48, of which waited for: 24 -> 22; matrix products, arithmetic and copies ran while one was open for 12% -> 12% of each run, Pallas kernels for 9% -> 9%
where the time goes in v3:
time: 219 us
  waiting for transfers between devices  123 us (56%)
  starting transfers between devices  29.1 us (13%)
  Pallas kernels  28.7 us (13%)
  matrix products  16.9 us (8%)
  local copies, waits for them, and re-layouts  13.7 us (6%)
  other arithmetic  7.05 us (3%)
    ppermute x27, waiting for transfers between devices, turned(): lax.ppermute(value, axis, [(i, (i + by) % length) for i in range(length)])  120 us
    ppermute x27, starting transfers between devices, turned(): lax.ppermute(value, axis, [(i, (i + by) % length) for i in range(length)])  18.8 us
    dot_general x10, matrix products, dot(): lax.dot_general(a, b, (((over[0],), (over[1],)), ((), ())), precision=pre...  16.9 us
    pallas_call x2, Pallas kernels, multiply_rows(): pl.pallas_call(product_rows, grid=(depth // block,), in_specs=[pl.BlockSp...  8.46 us
    unnamed x64, local copies, waits for them, and re-layouts  8.23 us
    ppermute x2, starting transfers between devices, shifted(): return lax.ppermute(value, axis, pairs)  7.38 us
    pallas_call x1, Pallas kernels, body(): pl.pallas_call(partial(backward_carried, heads, block), out_shape=[shape(...  5.11 us
    pallas_call x1, Pallas kernels, body(): pl.pallas_call(partial(forward_local, heads, block), out_shape=[shape(len...  4.79 us
  transfers between devices with their start and end apart: 48, of which 22 were waited for; matrix products, arithmetic and copies ran while one was open for 12% of the time, Pallas kernels for 9%

profile of v3, /device:TPU:4, one launch (start us, length us, event | category | flops | bytes accessed | tf_op | source)
XLA Modules:
  0.0 218.7 jit_solution(15105876637780735117)
XLA Ops:
  12.3 3.9 %collective-permute-done = bf16[48,4096]{1,0:T(8,128)(2,1)} collective-permute-done((bf16[48,4096]{1,0:T(8,128)(2,1)}, bf16[48,4096]{1,0:T(8,128)(2,1)}, u32[]{:S(2)}, u32[]{:S(2)}) %collective-permute-start) | collective-permute-done | bytes 393248 | tf_op jit(solution)/shard_map/ppermute | solution.py:305
  16.2 8.4 %collective-permute-done.2 = bf16[48,4096]{1,0:T(8,128)(2,1)} collective-permute-done((bf16[48,4096]{1,0:T(8,128)(2,1)S(1)}, bf16[48,4096]{1,0:T(8,128)(2,1)}, u32[]{:S(2)}, u32[]{:S(2)}) %collective-permute-start.2) | collective-permute-done | bytes 393248 | tf_op jit(solution)/shard_map/ppermute | solution.py:305
  24.6 5.5 %fusion.48 = bf16[192,896]{1,0:T(8,128)(2,1)S(1)} fusion(bf16[4096,896]{1,0:T(8,128)(2,1)} %fusion.1.weight, bf16[48,4096]{1,0:T(8,128)(2,1)} %collective-permute-done.20, bf16[48,4096]{1,0:T(8,128)(2,1)} %collective-permute-done.19, bf16[96,4096]{1,0:T(8,128)(2,1)} %param.11), kind=kOutput, calls=%fused_computation.51 | convolution fusion | flops 1414176768 | bytes 9256960 | tf_op jit(solution)/shard_map/dot_general | solution.py:28
  30.4 9.9 %collective-permute-done.3 = bf16[48,4096]{1,0:T(8,128)(2,1)S(1)} collective-permute-done((bf16[48,4096]{1,0:T(8,128)(2,1)}, bf16[48,4096]{1,0:T(8,128)(2,1)S(1)}, u32[]{:S(2)}, u32[]{:S(2)}) %collective-permute-start.3) | collective-permute-done | bytes 393248 | tf_op jit(solution)/shard_map/ppermute | solution.py:305
  45.2 8.9 %collective-permute-done.4 = bf16[48,4096]{1,0:T(8,128)(2,1)S(1)} collective-permute-done((bf16[48,4096]{1,0:T(8,128)(2,1)S(1)}, bf16[48,4096]{1,0:T(8,128)(2,1)S(1)}, u32[]{:S(2)}, u32[]{:S(2)}) %collective-permute-start.4) | collective-permute-done | bytes 393248 | tf_op jit(solution)/shard_map/ppermute | solution.py:305
  56.9 4.9 %collective-permute-done.26 = bf16[48,4096]{1,0:T(8,128)(2,1)S(1)} collective-permute-done((bf16[48,4096]{1,0:T(8,128)(2,1)S(1)}, bf16[48,4096]{1,0:T(8,128)(2,1)S(1)}, u32[]{:S(2)}, u32[]{:S(2)}) %collective-permute-start.26) | collective-permute-done | bytes 393248 | tf_op jit(solution)/shard_map/ppermute | solution.py:305
  64.9 5.4 %collective-permute-done.8 = bf16[48,4096]{1,0:T(8,128)(2,1)S(1)} collective-permute-done((bf16[48,4096]{1,0:T(8,128)(2,1)S(1)}, bf16[48,4096]{1,0:T(8,128)(2,1)S(1)}, u32[]{:S(2)}, u32[]{:S(2)}) %collective-permute-start.8) | collective-permute-done | bytes 393248 | tf_op jit(solution)/shard_map/ppermute | solution.py:305
  70.3 3.4 %collective-permute-start.28 = (bf16[8,512]{1,0:T(8,128)(2,1)S(1)}, bf16[8,512]{1,0:T(8,128)(2,1)S(1)}, u32[]{:S(2)}, u32[]{:S(2)}) collective-permute-start(bf16[8,512]{1,0:T(8,128)(2,1)S(1)} %slice_add_fusion.2), channel_id=1, source_target_pairs={{0,8},{8,16},{16,24},{1,9},{9,17},{17,25},{2,10},{10,18},{18,26},{... | collective-permute-start | bytes 24584 | tf_op jit(solution)/shard_map/ppermute | solution.py:316
  77.5 4.8 %forward_local.1 = (bf16[768,1280]{1,0:T(8,128)(2,1)S(1)}, f32[768,896]{1,0:T(8,128)S(1)}, f32[768,256]{1,0:T(8,128)S(1)}, f32[1536,128]{1,0:T(8,128)S(1)}, f32[256,128]{1,0:T(8,128)S(1)}) custom-call(bf16[768,896]{1,0:T(8,128)(2,1)S(1)} %slice_dynamic-update-slice_fusion.12.proj, bf16[8,512]{1,0:T(8,128)(2,1)S(1)} %broadcast_add_fusion.tail, ...), custom_call_target="tpu_custom_call" | custom-call | flops 1000 | bytes 1000 | tf_op jit(solution)/shard_map/forward_local/pallas_call | solution.py:455
  82.4 5.2 %collective-permute-done.12 = bf16[48,4096]{1,0:T(8,128)(2,1)S(1)} collective-permute-done((bf16[48,4096]{1,0:T(8,128)(2,1)S(1)}, bf16[48,4096]{1,0:T(8,128)(2,1)S(1)}, u32[]{:S(2)}, u32[]{:S(2)}) %collective-permute-start.12) | collective-permute-done | bytes 393248 | tf_op jit(solution)/shard_map/ppermute | solution.py:305
  91.1 4.9 %collective-permute-done.11 = bf16[48,4096]{1,0:T(8,128)(2,1)S(1)} collective-permute-done((bf16[48,4096]{1,0:T(8,128)(2,1)S(1)}, bf16[48,4096]{1,0:T(8,128)(2,1)S(1)}, u32[]{:S(2)}, u32[]{:S(2)}) %collective-permute-start.11) | collective-permute-done | bytes 393248 | tf_op jit(solution)/shard_map/ppermute | solution.py:305
  97.2 15.2 %collective-permute-done.15 = bf16[48,4096]{1,0:T(8,128)(2,1)S(1)} collective-permute-done((bf16[48,4096]{1,0:T(8,128)(2,1)S(1)}, bf16[48,4096]{1,0:T(8,128)(2,1)S(1)}, u32[]{:S(2)}, u32[]{:S(2)}) %collective-permute-start.15) | collective-permute-done | bytes 393248 | tf_op jit(solution)/shard_map/ppermute | solution.py:305
  113.8 3.5 %forward_carried.1 = (f32[768,768]{1,0:T(8,128)S(1)}, bf16[768,512]{1,0:T(8,128)(2,1)S(1)}, f32[8,768]{1,0:T(8,128)S(1)}) custom-call(bf16[768,896]{1,0:T(8,128)(2,1)S(1)} %slice_dynamic-update-slice_fusion.12.proj, bf16[768,1280]{1,0:T(8,128)(2,1)S(1)} %get-tuple-element.23.saved, f32[768,896]{1,0:T(8,128)S(1)} %get-tuple-element.24.factors, ...), custom_call_target="tpu_custom_call" | custom-call | flops 1000 | bytes 1000 | tf_op jit(solution)/shard_map/forward_carried/pallas_call | solution.py:493
  121.2 3.7 %collective-permute-start.35 = (f32[8,768]{1,0:T(8,128)S(1)}, f32[8,768]{1,0:T(8,128)S(1)}, u32[]{:S(2)}, u32[]{:S(2)}) collective-permute-start(f32[8,768]{1,0:T(8,128)S(1)} %add.458.refs_0_), channel_id=1, source_target_pairs={{0,6},{1,7},{2,0},{3,1},{4,2},{5,3},{6,4},{7,5},{8,14},{9,15},{10,... | collective-permute-start | bytes 73736 | tf_op jit(solution)/shard_map/ppermute | solution.py:305
  140.3 5.1 %backward_carried.1 = (bf16[768,896]{1,0:T(8,128)(2,1)S(1)}, f32[8,512]{1,0:T(8,128)S(1)}, f32[8,512]{1,0:T(8,128)}) custom-call(bf16[768,768]{1,0:T(8,128)(2,1)S(1)} %get-tuple-element.30.cots, bf16[768,1280]{1,0:T(8,128)(2,1)S(1)} %copy-done.5, f32[768,896]{1,0:T(8,128)S(1)} %copy-done.7, f32[1,128]{1,0:T(1,128)S(1)} %get-tuple-element.51.rate, ...), custom_call_target="tpu_custom_call" | custom-call | flops 1000 | bytes 1000 | tf_op jit(solution)/shard_map/backward_carried/pallas_call | solution.py:531
  146.0 4.0 %collective-permute-start.40 = (f32[8,512]{1,0:T(8,128)}, f32[8,512]{1,0:T(8,128)S(1)}, u32[]{:S(2)}, u32[]{:S(2)}) collective-permute-start(f32[8,512]{1,0:T(8,128)} %get-tuple-element.38), channel_id=1, source_target_pairs={{8,0},{16,8},{24,16},{9,1},{17,9},{25,17},{10,2},{18,10},{26,18},{... | collective-permute-start | bytes 49160 | tf_op jit(solution)/shard_map/ppermute | solution.py:316
  153.1 4.2 %product_rows.2 = (bf16[192,4096]{1,0:T(8,128)(2,1)S(1)}, bf16[192,4096]{1,0:T(8,128)(2,1)S(1)}) custom-call(bf16[384,896]{1,0:T(8,128)(2,1)S(1)} %dynamic-slice_dynamic-update-slice_fusion.8.rows, bf16[4096,896]{1,0:T(8,128)(2,1)S(1)} %copy-done.2), custom_call_target="tpu_custom_call" | custom-call | flops 1000 | bytes 1000 | tf_op jit(solution)/shard_map/product_rows/pallas_call | solution.py:374
  157.7 4.2 %product_rows.3 = (bf16[192,4096]{1,0:T(8,128)(2,1)S(1)}, bf16[192,4096]{1,0:T(8,128)(2,1)S(1)}) custom-call(bf16[384,896]{1,0:T(8,128)(2,1)S(1)} %dynamic-slice_dynamic-update-slice_fusion.rows, bf16[4096,896]{1,0:T(8,128)(2,1)S(1)} %copy-done.2), custom_call_target="tpu_custom_call" | custom-call | flops 1000 | bytes 1000 | tf_op jit(solution)/shard_map/product_rows/pallas_call | solution.py:374
  167.7 8.7 %collective-permute-done.42 = bf16[48,4096]{1,0:T(8,128)(2,1)S(1)} collective-permute-done((bf16[48,4096]{1,0:T(8,128)(2,1)S(1)}, bf16[48,4096]{1,0:T(8,128)(2,1)S(1)}, u32[]{:S(2)}, u32[]{:S(2)}) %collective-permute-start.42) | collective-permute-done | bytes 393248 | tf_op jit(solution)/shard_map/ppermute | solution.py:305
  176.9 8.0 %collective-permute-done.45 = bf16[48,4096]{1,0:T(8,128)(2,1)S(1)} collective-permute-done((bf16[48,4096]{1,0:T(8,128)(2,1)S(1)}, bf16[48,4096]{1,0:T(8,128)(2,1)S(1)}, u32[]{:S(2)}, u32[]{:S(2)}) %collective-permute-start.45) | collective-permute-done | bytes 393248 | tf_op jit(solution)/shard_map/ppermute | solution.py:305
  185.3 8.0 %collective-permute-done.43 = bf16[48,4096]{1,0:T(8,128)(2,1)S(1)} collective-permute-done((bf16[48,4096]{1,0:T(8,128)(2,1)S(1)}, bf16[48,4096]{1,0:T(8,128)(2,1)S(1)}, u32[]{:S(2)}, u32[]{:S(2)}) %collective-permute-start.43) | collective-permute-done | bytes 393248 | tf_op jit(solution)/shard_map/ppermute | solution.py:305
  193.7 8.0 %collective-permute-done.46 = bf16[48,4096]{1,0:T(8,128)(2,1)S(1)} collective-permute-done((bf16[48,4096]{1,0:T(8,128)(2,1)S(1)}, bf16[48,4096]{1,0:T(8,128)(2,1)S(1)}, u32[]{:S(2)}, u32[]{:S(2)}) %collective-permute-start.46) | collective-permute-done | bytes 393248 | tf_op jit(solution)/shard_map/ppermute | solution.py:305
  202.1 8.0 %collective-permute-done.44 = bf16[48,4096]{1,0:T(8,128)(2,1)S(1)} collective-permute-done((bf16[48,4096]{1,0:T(8,128)(2,1)S(1)}, bf16[48,4096]{1,0:T(8,128)(2,1)S(1)}, u32[]{:S(2)}, u32[]{:S(2)}) %collective-permute-start.44) | collective-permute-done | bytes 393248 | tf_op jit(solution)/shard_map/ppermute | solution.py:305
  210.3 7.4 %collective-permute-done.47 = bf16[48,4096]{1,0:T(8,128)(2,1)S(1)} collective-permute-done((bf16[48,4096]{1,0:T(8,128)(2,1)S(1)}, bf16[48,4096]{1,0:T(8,128)(2,1)S(1)}, u32[]{:S(2)}, u32[]{:S(2)}) %collective-permute-start.47) | collective-permute-done | bytes 393248 | tf_op jit(solution)/shard_map/ppermute | solution.py:305
  (218 shorter events, 64.7 us)
Async XLA Ops:
  2.1 14.1 %collective-permute-start = (bf16[48,4096]{1,0:T(8,128)(2,1)}, bf16[48,4096]{1,0:T(8,128)(2,1)}, u32[]{:S(2)}, u32[]{:S(2)}) collective-permute-start(bf16[48,4096]{1,0:T(8,128)(2,1)} %get-tuple-element.45), channel_id=1, source_target_pairs={{0,2},{1,3},{2,4},{3,5},{4,6},{5,7},{6,0},{7,1},{8,10},{9,11},{10,... | collective-permute-start | bytes 1179656 | tf_op jit(solution)/shard_map/ppermute | solution.py:305
  3.7 21.0 %collective-permute-start.20 = (bf16[48,4096]{1,0:T(8,128)(2,1)}, bf16[48,4096]{1,0:T(8,128)(2,1)}, u32[]{:S(2)}, u32[]{:S(2)}) collective-permute-start(bf16[48,4096]{1,0:T(8,128)(2,1)} %get-tuple-element.45), channel_id=1, source_target_pairs={{0,1},{1,0},{2,3},{3,2},{4,5},{5,4},{6,7},{7,6},{8,9},{9,8},{10,11... | collective-permute-start | bytes 1179656 | tf_op jit(solution)/shard_map/ppermute | solution.py:310
  3.7 21.0 %collective-permute-start.2 = (bf16[48,4096]{1,0:T(8,128)(2,1)S(1)}, bf16[48,4096]{1,0:T(8,128)(2,1)}, u32[]{:S(2)}, u32[]{:S(2)}) collective-permute-start(bf16[48,4096]{1,0:T(8,128)(2,1)S(1)} %get-tuple-element.46), channel_id=1, source_target_pairs={{0,2},{1,3},{2,4},{3,5},{4,6},{5,7},{6,0},{7,1},{8,10},{9,11},{10,... | collective-permute-start | bytes 1179656 | tf_op jit(solution)/shard_map/ppermute | solution.py:305
  5.2 19.4 %collective-permute-start.19 = (bf16[48,4096]{1,0:T(8,128)(2,1)S(1)}, bf16[48,4096]{1,0:T(8,128)(2,1)}, u32[]{:S(2)}, u32[]{:S(2)}) collective-permute-start(bf16[48,4096]{1,0:T(8,128)(2,1)S(1)} %get-tuple-element.46), channel_id=1, source_target_pairs={{0,1},{1,0},{2,3},{3,2},{4,5},{5,4},{6,7},{7,6},{8,9},{9,8},{10,11... | collective-permute-start | bytes 1179656 | tf_op jit(solution)/shard_map/ppermute | solution.py:310
  16.2 27.2 %collective-permute-start.1 = (bf16[48,4096]{1,0:T(8,128)(2,1)}, bf16[48,4096]{1,0:T(8,128)(2,1)S(1)}, u32[]{:S(2)}, u32[]{:S(2)}) collective-permute-start(bf16[48,4096]{1,0:T(8,128)(2,1)} %collective-permute-done), channel_id=1, source_target_pairs={{0,2},{1,3},{2,4},{3,5},{4,6},{5,7},{6,0},{7,1},{8,10},{9,11},{10,... | collective-permute-start | bytes 1179656 | tf_op jit(solution)/shard_map/ppermute | solution.py:305
  16.2 24.1 %collective-permute-start.22 = (bf16[48,4096]{1,0:T(8,128)(2,1)}, bf16[48,4096]{1,0:T(8,128)(2,1)S(1)}, u32[]{:S(2)}, u32[]{:S(2)}) collective-permute-start(bf16[48,4096]{1,0:T(8,128)(2,1)} %collective-permute-done), channel_id=1, source_target_pairs={{0,1},{1,0},{2,3},{3,2},{4,5},{5,4},{6,7},{7,6},{8,9},{9,8},{10,11... | collective-permute-start | bytes 1179656 | tf_op jit(solution)/shard_map/ppermute | solution.py:310
  24.6 15.7 %collective-permute-start.3 = (bf16[48,4096]{1,0:T(8,128)(2,1)}, bf16[48,4096]{1,0:T(8,128)(2,1)S(1)}, u32[]{:S(2)}, u32[]{:S(2)}) collective-permute-start(bf16[48,4096]{1,0:T(8,128)(2,1)} %collective-permute-done.2), channel_id=1, source_target_pairs={{0,2},{1,3},{2,4},{3,5},{4,6},{5,7},{6,0},{7,1},{8,10},{9,11},{10,... | collective-permute-start | bytes 1179656 | tf_op jit(solution)/shard_map/ppermute | solution.py:305
  24.6 15.7 %collective-permute-start.21 = (bf16[48,4096]{1,0:T(8,128)(2,1)}, bf16[48,4096]{1,0:T(8,128)(2,1)S(1)}, u32[]{:S(2)}, u32[]{:S(2)}) collective-permute-start(bf16[48,4096]{1,0:T(8,128)(2,1)} %collective-permute-done.2), channel_id=1, source_target_pairs={{0,1},{1,0},{2,3},{3,2},{4,5},{5,4},{6,7},{7,6},{8,9},{9,8},{10,11... | collective-permute-start | bytes 1179656 | tf_op jit(solution)/shard_map/ppermute | solution.py:310
  43.9 18.0 %collective-permute-start.26 = (bf16[48,4096]{1,0:T(8,128)(2,1)S(1)}, bf16[48,4096]{1,0:T(8,128)(2,1)S(1)}, u32[]{:S(2)}, u32[]{:S(2)}) collective-permute-start(bf16[48,4096]{1,0:T(8,128)(2,1)S(1)} %collective-permute-done.1), channel_id=1, source_target_pairs={{0,2},{1,3},{2,4},{3,5},{4,6},{5,7},{6,0},{7,1},{8,10},{9,11},{10,... | collective-permute-start | bytes 1179656 | tf_op jit(solution)/shard_map/ppermute | solution.py:305
  54.3 19.5 %collective-permute-start.6 = (bf16[48,4096]{1,0:T(8,128)(2,1)S(1)}, bf16[48,4096]{1,0:T(8,128)(2,1)S(1)}, u32[]{:S(2)}, u32[]{:S(2)}) collective-permute-start(bf16[48,4096]{1,0:T(8,128)(2,1)S(1)} %get-tuple-element.44), channel_id=1, source_target_pairs={{0,1},{1,0},{2,3},{3,2},{4,5},{5,4},{6,7},{7,6},{8,9},{9,8},{10,11... | collective-permute-start | bytes 1179656 | tf_op jit(solution)/shard_map/ppermute | solution.py:310
  54.3 15.9 %collective-permute-start.8 = (bf16[48,4096]{1,0:T(8,128)(2,1)S(1)}, bf16[48,4096]{1,0:T(8,128)(2,1)S(1)}, u32[]{:S(2)}, u32[]{:S(2)}) collective-permute-start(bf16[48,4096]{1,0:T(8,128)(2,1)S(1)} %get-tuple-element.44), channel_id=1, source_target_pairs={{0,2},{1,3},{2,4},{3,5},{4,6},{5,7},{6,0},{7,1},{8,10},{9,11},{10,... | collective-permute-start | bytes 1179656 | tf_op jit(solution)/shard_map/ppermute | solution.py:305
  54.4 19.4 %collective-permute-start.5 = (bf16[48,4096]{1,0:T(8,128)(2,1)S(1)}, bf16[48,4096]{1,0:T(8,128)(2,1)S(1)}, u32[]{:S(2)}, u32[]{:S(2)}) collective-permute-start(bf16[48,4096]{1,0:T(8,128)(2,1)S(1)} %get-tuple-element.43), channel_id=1, source_target_pairs={{0,1},{1,0},{2,3},{3,2},{4,5},{5,4},{6,7},{7,6},{8,9},{9,8},{10,11... | collective-permute-start | bytes 1179656 | tf_op jit(solution)/shard_map/ppermute | solution.py:310
  61.8 15.6 %collective-permute-start.7 = (bf16[48,4096]{1,0:T(8,128)(2,1)S(1)}, bf16[48,4096]{1,0:T(8,128)(2,1)S(1)}, u32[]{:S(2)}, u32[]{:S(2)}) collective-permute-start(bf16[48,4096]{1,0:T(8,128)(2,1)S(1)} %get-tuple-element.43), channel_id=1, source_target_pairs={{0,2},{1,3},{2,4},{3,5},{4,6},{5,7},{6,0},{7,1},{8,10},{9,11},{10,... | collective-permute-start | bytes 1179656 | tf_op jit(solution)/shard_map/ppermute | solution.py:305
  73.7 16.0 %collective-permute-start.10 = (bf16[48,4096]{1,0:T(8,128)(2,1)S(1)}, bf16[48,4096]{1,0:T(8,128)(2,1)S(1)}, u32[]{:S(2)}, u32[]{:S(2)}) collective-permute-start(bf16[48,4096]{1,0:T(8,128)(2,1)S(1)} %collective-permute-done.8), channel_id=1, source_target_pairs={{0,1},{1,0},{2,3},{3,2},{4,5},{5,4},{6,7},{7,6},{8,9},{9,8},{10,11... | collective-permute-start | bytes 1179656 | tf_op jit(solution)/shard_map/ppermute | solution.py:310
  77.4 18.6 %collective-permute-start.11 = (bf16[48,4096]{1,0:T(8,128)(2,1)S(1)}, bf16[48,4096]{1,0:T(8,128)(2,1)S(1)}, u32[]{:S(2)}, u32[]{:S(2)}) collective-permute-start(bf16[48,4096]{1,0:T(8,128)(2,1)S(1)} %collective-permute-done.7), channel_id=1, source_target_pairs={{0,2},{1,3},{2,4},{3,5},{4,6},{5,7},{6,0},{7,1},{8,10},{9,11},{10,... | collective-permute-start | bytes 1179656 | tf_op jit(solution)/shard_map/ppermute | solution.py:305
  90.2 22.2 %collective-permute-start.17 = (bf16[48,4096]{1,0:T(8,128)(2,1)S(1)}, bf16[48,4096]{1,0:T(8,128)(2,1)S(1)}, u32[]{:S(2)}, u32[]{:S(2)}) collective-permute-start(bf16[48,4096]{1,0:T(8,128)(2,1)S(1)} %collective-permute-done.12), channel_id=1, source_target_pairs={{0,2},{1,3},{2,4},{3,5},{4,6},{5,7},{6,0},{7,1},{8,10},{9,11},{10,... | collective-permute-start | bytes 1179656 | tf_op jit(solution)/shard_map/ppermute | solution.py:305
  96.0 16.4 %collective-permute-start.15 = (bf16[48,4096]{1,0:T(8,128)(2,1)S(1)}, bf16[48,4096]{1,0:T(8,128)(2,1)S(1)}, u32[]{:S(2)}, u32[]{:S(2)}) collective-permute-start(bf16[48,4096]{1,0:T(8,128)(2,1)S(1)} %collective-permute-done.11), channel_id=1, source_target_pairs={{0,2},{1,3},{2,4},{3,5},{4,6},{5,7},{6,0},{7,1},{8,10},{9,11},{10,... | collective-permute-start | bytes 1179656 | tf_op jit(solution)/shard_map/ppermute | solution.py:305
  96.0 17.0 %collective-permute-start.14 = (bf16[48,4096]{1,0:T(8,128)(2,1)S(1)}, bf16[48,4096]{1,0:T(8,128)(2,1)S(1)}, u32[]{:S(2)}, u32[]{:S(2)}) collective-permute-start(bf16[48,4096]{1,0:T(8,128)(2,1)S(1)} %collective-permute-done.12), channel_id=1, source_target_pairs={{0,1},{1,0},{2,3},{3,2},{4,5},{5,4},{6,7},{7,6},{8,9},{9,8},{10,11... | collective-permute-start | bytes 1179656 | tf_op jit(solution)/shard_map/ppermute | solution.py:310
  96.4 16.6 %collective-permute-start.13 = (bf16[48,4096]{1,0:T(8,128)(2,1)S(1)}, bf16[48,4096]{1,0:T(8,128)(2,1)S(1)}, u32[]{:S(2)}, u32[]{:S(2)}) collective-permute-start(bf16[48,4096]{1,0:T(8,128)(2,1)S(1)} %collective-permute-done.11), channel_id=1, source_target_pairs={{0,1},{1,0},{2,3},{3,2},{4,5},{5,4},{6,7},{7,6},{8,9},{9,8},{10,11... | collective-permute-start | bytes 1179656 | tf_op jit(solution)/shard_map/ppermute | solution.py:310
  165.6 19.2 %collective-permute-start.45 = (bf16[48,4096]{1,0:T(8,128)(2,1)S(1)}, bf16[48,4096]{1,0:T(8,128)(2,1)S(1)}, u32[]{:S(2)}, u32[]{:S(2)}) collective-permute-start(bf16[48,4096]{1,0:T(8,128)(2,1)S(1)} %add_convert_fusion.7), channel_id=1, source_target_pairs={{0,2},{1,3},{2,4},{3,5},{4,6},{5,7},{6,0},{7,1},{8,10},{9,11},{10,... | collective-permute-start | bytes 1179656 | tf_op jit(solution)/shard_map/ppermute | solution.py:305
  176.6 16.7 %collective-permute-start.43 = (bf16[48,4096]{1,0:T(8,128)(2,1)S(1)}, bf16[48,4096]{1,0:T(8,128)(2,1)S(1)}, u32[]{:S(2)}, u32[]{:S(2)}) collective-permute-start(bf16[48,4096]{1,0:T(8,128)(2,1)S(1)} %add_convert_fusion.5), channel_id=1, source_target_pairs={{0,2},{1,3},{2,4},{3,5},{4,6},{5,7},{6,0},{7,1},{8,10},{9,11},{10,... | collective-permute-start | bytes 1179656 | tf_op jit(solution)/shard_map/ppermute | solution.py:305
  185.0 16.7 %collective-permute-start.46 = (bf16[48,4096]{1,0:T(8,128)(2,1)S(1)}, bf16[48,4096]{1,0:T(8,128)(2,1)S(1)}, u32[]{:S(2)}, u32[]{:S(2)}) collective-permute-start(bf16[48,4096]{1,0:T(8,128)(2,1)S(1)} %add_convert_fusion.2), channel_id=1, source_target_pairs={{0,2},{1,3},{2,4},{3,5},{4,6},{5,7},{6,0},{7,1},{8,10},{9,11},{10,... | collective-permute-start | bytes 1179656 | tf_op jit(solution)/shard_map/ppermute | solution.py:305
  193.4 16.7 %collective-permute-start.44 = (bf16[48,4096]{1,0:T(8,128)(2,1)S(1)}, bf16[48,4096]{1,0:T(8,128)(2,1)S(1)}, u32[]{:S(2)}, u32[]{:S(2)}) collective-permute-start(bf16[48,4096]{1,0:T(8,128)(2,1)S(1)} %add_convert_fusion.4), channel_id=1, source_target_pairs={{0,2},{1,3},{2,4},{3,5},{4,6},{5,7},{6,0},{7,1},{8,10},{9,11},{10,... | collective-permute-start | bytes 1179656 | tf_op jit(solution)/shard_map/ppermute | solution.py:305
  201.8 15.8 %collective-permute-start.47 = (bf16[48,4096]{1,0:T(8,128)(2,1)S(1)}, bf16[48,4096]{1,0:T(8,128)(2,1)S(1)}, u32[]{:S(2)}, u32[]{:S(2)}) collective-permute-start(bf16[48,4096]{1,0:T(8,128)(2,1)S(1)} %add_convert_fusion.1), channel_id=1, source_target_pairs={{0,2},{1,3},{2,4},{3,5},{4,6},{5,7},{6,0},{7,1},{8,10},{9,11},{10,... | collective-permute-start | bytes 1179656 | tf_op jit(solution)/shard_map/ppermute | solution.py:305
  (48 other events, 444.7 us)
